TPU v7x, 128 devices: a whole 4x4x4 slice. The times are simulated.
128 devices in a mesh: frame: 64 (over x_hi, y, z, core), video: 2 (over x_lo).
Axes of the slice: x: 4 (x_hi: 2, x_lo: 2; x = x_hi * 2 + x_lo), y: 4, z: 4, core: 2. Of those that a mesh axis runs over, the one named last changes fastest.
Arguments:
- tokens_in: bfloat16 [2, 256, 197, 768], P('video', 'frame'), may hold values from -6 to 6
- clip_ids: int32 [2, 256], P('video', 'frame'), may hold values from 0 to 7, as said below
- grad_out: bfloat16 [2, 256, 197, 768], P('video', 'frame'), may hold values from -6 to 6
- msg_fc_w: bfloat16 [768, 768], P('frame'), may hold values from -0.21875 to 0.21875
- msg_fc_b: bfloat16 [768], P('frame'), may hold values from -1.75 to 1.75
- msg_norm_gain: bfloat16 [768], P('frame'), may hold values from 0.5 to 1.5
- msg_norm_shift: bfloat16 [768], P('frame'), may hold values from -1.75 to 1.75
- msg_qkv_w: bfloat16 [768, 2304], P('frame'), may hold values from -0.21875 to 0.21875
- msg_qv_b: bfloat16 [1536], P('frame'), may hold values from -1.75 to 1.75
- msg_out_w: bfloat16 [768, 768], P('frame'), may hold values from -0.4375 to 0.4375
- msg_out_b: bfloat16 [768], P('frame'), may hold values from -1.75 to 1.75
- norm1_gain: bfloat16 [768], P('frame'), may hold values from 0.5 to 1.5
- norm1_shift: bfloat16 [768], P('frame'), may hold values from -1.75 to 1.75
- attn_qkv_w: bfloat16 [768, 2304], P('frame'), may hold values from -0.21875 to 0.21875
- attn_qv_b: bfloat16 [1536], P('frame'), may hold values from -1.75 to 1.75
- attn_out_w: bfloat16 [768, 768], P('frame'), may hold values from -0.625 to 0.625
- attn_out_b: bfloat16 [768], P('frame'), may hold values from -1.75 to 1.75
- norm2_gain: bfloat16 [768], P('frame'), may hold values from 0.5 to 1.5
- norm2_shift: bfloat16 [768], P('frame'), may hold values from -1.75 to 1.75
- mlp_in_w: bfloat16 [768, 3072], P('frame'), may hold values from -0.21875 to 0.21875
- mlp_in_b: bfloat16 [3072], P('frame'), may hold values from -1.75 to 1.75
- mlp_out_w: bfloat16 [3072, 768], P('frame'), may hold values from -0.109375 to 0.109375
- mlp_out_b: bfloat16 [768], P('frame'), may hold values from -1.75 to 1.75
Outputs:
- layer_out: bfloat16 [2, 256, 197, 768], P('video', 'frame')
- grad_tokens: float32 [2, 256, 197, 768], P('video', 'frame')
- grad_msg_fc_w: float32 [768, 768], P('frame')
- grad_msg_fc_b: float32 [768], P('frame')
- grad_msg_norm_gain: float32 [768], P('frame')
- grad_msg_norm_shift: float32 [768], P('frame')
- grad_msg_qkv_w: float32 [768, 2304], P('frame')
- grad_msg_qv_b: float32 [1536], P('frame')
- grad_msg_out_w: float32 [768, 768], P('frame')
- grad_msg_out_b: float32 [768], P('frame')
- grad_norm1_gain: float32 [768], P('frame')
- grad_norm1_shift: float32 [768], P('frame')
- grad_attn_qkv_w: float32 [768, 2304], P('frame')
- grad_attn_qv_b: float32 [1536], P('frame')
- grad_attn_out_w: float32 [768, 768], P('frame')
- grad_attn_out_b: float32 [768], P('frame')
- grad_norm2_gain: float32 [768], P('frame')
- grad_norm2_shift: float32 [768], P('frame')
- grad_mlp_in_w: float32 [768, 3072], P('frame')
- grad_mlp_in_b: float32 [3072], P('frame')
- grad_mlp_out_w: float32 [3072, 768], P('frame')
- grad_mlp_out_b: float32 [768], P('frame')
Inputs may be any that keep to these rules, and one draw needn't show every extreme that they name: `clip_ids`: in every video, frame 0, frame 256 // 2 and the last frame share one clip group drawn from the seed.
All inputs are finite; a program needn't handle non-finite values.
Results may differ from a plain program's by a relative error of at most 0.03.
Values may be sent and summed in bfloat16 or wider, within the bound.
No kernel may reach another device: no remote copies, remote signals or barrier semaphores. Data moves between devices by JAX's collectives and lax.ppermute only.
A program may use at most 256 MiB of HBM per device.

v0:
```python
import math

import jax
import jax.numpy as jnp
from jax import lax
from jax.sharding import PartitionSpec as P

HEAD_DIM = 64


def in_one_piece(arrays, axis, dim, along):
    widths = [math.prod(a.shape[along:]) for a in arrays]
    both = jnp.concatenate(
        [a.reshape(*a.shape[:along], w) for a, w in zip(arrays, widths)], axis=along
    )
    result = lax.all_gather(both, axis, axis=dim, tiled=True)
    parts = jnp.split(result, [sum(widths[:k]) for k in range(1, len(widths))], axis=along)
    return tuple(
        (b.reshape(*result.shape[:along], *a.shape[along:]) for a, b in zip(arrays, parts))
    )


def side_by_side(arrays, axis, dim, along):
    widths = [a.shape[along] for a in arrays]
    both = jnp.concatenate(arrays, axis=along)
    result = lax.all_gather(both, axis, axis=dim, tiled=True)
    return tuple(jnp.split(result, [sum(widths[:k]) for k in range(1, len(widths))], axis=along))


def split_up(x, dim, length):
    shape = x.shape
    parts = x.reshape(*shape[:dim], length, shape[dim] // length, *shape[dim + 1 :])
    return jnp.moveaxis(parts, dim, 0)


def one_scatter(arrays, axis, dims):
    length = lax.axis_size(axis)
    parts = [split_up(a, dim, length) for a, dim in zip(arrays, dims)]
    lines = jnp.concatenate([b.reshape(length, -1) for b in parts], axis=1)
    span = max(16, -(-lines.shape[1] // 1024) * 8)
    lines = jnp.pad(lines, ((0, 0), (0, span * 128 - lines.shape[1]))).reshape(-1, 128)
    ravelled, at, done = (lax.psum_scatter(lines, axis, tiled=True).reshape(-1), 0, [])
    for b in parts:
        part = b[0]
        done.append(ravelled[at : at + part.size].reshape(part.shape))
        at += part.size
    return tuple(done)


def sent_to_all(x, axis):
    length = lax.axis_size(axis)
    return lax.all_to_all(jnp.broadcast_to(x[None], (length, *x.shape)), axis, 0, 0, tiled=True)


def taken_together(x, axis):
    everything = sent_to_all(x, axis)
    return jnp.sum(everything.astype(jnp.float32), axis=0)


def narrow(value):
    return value.astype(jnp.bfloat16)


def product(left, right):
    return jnp.dot(left, right, preferred_element_type=jnp.float32)


def product_left_t(left, right):
    return lax.dot_general(
        left, right, (((0,), (0,)), ((), ())), preferred_element_type=jnp.float32
    )


def product_right_t(left, right):
    return lax.dot_general(
        left, right, (((1,), (1,)), ((), ())), preferred_element_type=jnp.float32
    )


def norm_parts(value):
    center = value - jnp.mean(value, -1, keepdims=True)
    inverse = lax.rsqrt(jnp.mean(center * center, -1, keepdims=True) + 1e-05)
    return (center * inverse, inverse)


def norm_back(grad_normed, normed, inverse, gain):
    scaled = grad_normed * gain
    return inverse * (
        scaled
        - jnp.mean(scaled, -1, keepdims=True)
        - normed * jnp.mean(scaled * normed, -1, keepdims=True)
    )


def softmax_rows(scores):
    peak = jnp.max(scores, -1, keepdims=True)
    raised = jnp.exp(scores - peak)
    return raised / jnp.sum(raised, -1, keepdims=True)


def column_sums(value):
    return jnp.sum(value.astype(jnp.float32), 0)


def shards(
    tokens_in,
    clip_ids,
    grad_out,
    msg_fc_w,
    msg_fc_b,
    msg_norm_gain,
    msg_norm_shift,
    msg_qkv_w,
    msg_qv_b,
    msg_out_w,
    msg_out_b,
    norm1_gain,
    norm1_shift,
    attn_qkv_w,
    attn_qv_b,
    attn_out_w,
    attn_out_b,
    norm2_gain,
    norm2_shift,
    mlp_in_w,
    mlp_in_b,
    mlp_out_w,
    mlp_out_b,
):
    gathered = (
        *in_one_piece(
            (msg_fc_w, msg_fc_b, msg_norm_gain, msg_norm_shift, msg_qkv_w), "frame", 0, 1
        ),
        lax.all_gather(msg_qv_b, "frame", axis=0, tiled=True),
        *in_one_piece((msg_out_w, msg_out_b, norm1_gain, norm1_shift, attn_qkv_w), "frame", 0, 1),
        lax.all_gather(attn_qv_b, "frame", axis=0, tiled=True),
        *in_one_piece((attn_out_w, attn_out_b, norm2_gain, norm2_shift, mlp_in_w), "frame", 0, 1),
        *in_one_piece((mlp_in_b, mlp_out_w), "frame", 0, 1),
        lax.all_gather(mlp_out_b, "frame", axis=0, tiled=True),
    )
    (
        fc_weight,
        fc_bias,
        mnorm_gain,
        mnorm_shift,
        mqkv_weight,
        mqv_bias,
        mout_weight,
        mout_bias,
        gain_one,
        shift_one,
        qkv_weight,
        qv_bias,
        out_weight,
        out_bias,
        gain_two,
        shift_two,
        up_weight,
        up_bias,
        down_weight,
        down_bias,
    ) = gathered
    model_width = tokens_in.shape[-1]
    head_count = model_width // HEAD_DIM
    frames_here = tokens_in.shape[1]
    token_count = tokens_in.shape[2]
    length = token_count + 1
    score_factor = HEAD_DIM ** (-0.5)
    inputs = tokens_in[0]
    groups = clip_ids[0]
    wide = jnp.float32
    class_rows = inputs[:, 0, :]
    message = product(class_rows, fc_weight) + fc_bias.astype(wide)
    msg_normed, msg_inverse = norm_parts(message)
    msg_input = narrow(msg_normed * mnorm_gain.astype(wide) + mnorm_shift.astype(wide))
    msg_project = product(msg_input, mqkv_weight)
    msg_query = narrow(msg_project[:, :model_width] + mqv_bias[:model_width].astype(wide))
    msg_key = narrow(msg_project[:, model_width : 2 * model_width])
    msg_value = narrow(msg_project[:, 2 * model_width :] + mqv_bias[model_width:].astype(wide))
    key_all, value_all, group_all = (
        *side_by_side((msg_key, msg_value), "frame", 0, 1),
        lax.all_gather(groups, "frame", axis=0, tiled=True),
    )
    frame_total = key_all.shape[0]
    query_heads = msg_query.reshape(frames_here, head_count, HEAD_DIM)
    key_heads = key_all.reshape(frame_total, head_count, HEAD_DIM)
    value_heads = value_all.reshape(frame_total, head_count, HEAD_DIM)
    same_group = (groups[:, None] == group_all[None, :])[None]
    msg_scores = (
        jnp.einsum("qhd,khd->hqk", query_heads, key_heads, preferred_element_type=wide)
        * score_factor
    )
    msg_scores = jnp.where(same_group, msg_scores, -1000000000.0)
    msg_probs = softmax_rows(msg_scores)
    msg_probs_low = narrow(msg_probs)
    msg_mixed = narrow(
        jnp.einsum("hqk,khd->qhd", msg_probs_low, value_heads, preferred_element_type=wide).reshape(
            frames_here, model_width
        )
    )
    message_token = message + product(msg_mixed, mout_weight) + mout_bias.astype(wide)
    joined = jnp.concatenate([inputs.astype(wide), message_token[:, None, :]], axis=1)
    normed_one, inverse_one = norm_parts(joined)
    block_input = narrow(normed_one * gain_one.astype(wide) + shift_one.astype(wide)).reshape(
        frames_here * length, model_width
    )
    project = product(block_input, qkv_weight)
    head_shape = (frames_here, length, head_count, HEAD_DIM)
    queries = narrow(project[:, :model_width] + qv_bias[:model_width].astype(wide)).reshape(
        head_shape
    )
    key_rows = narrow(project[:, model_width : 2 * model_width]).reshape(head_shape)
    value_rows = narrow(project[:, 2 * model_width :] + qv_bias[model_width:].astype(wide)).reshape(
        head_shape
    )
    scores = (
        jnp.einsum("fqhd,fkhd->fhqk", queries, key_rows, preferred_element_type=wide) * score_factor
    )
    attn_probs = softmax_rows(scores)
    probs_low = narrow(attn_probs)
    mixed_rows = narrow(
        jnp.einsum("fhqk,fkhd->fqhd", probs_low, value_rows, preferred_element_type=wide).reshape(
            frames_here * length, model_width
        )
    )
    branch = product(mixed_rows, out_weight) + out_bias.astype(wide)
    residual = joined + branch.reshape(frames_here, length, model_width)
    kept = residual[:, :token_count]
    normed_two, inverse_two = norm_parts(kept)
    mlp_input = narrow(normed_two * gain_two.astype(wide) + shift_two.astype(wide)).reshape(
        frames_here * token_count, model_width
    )
    hidden = product(mlp_input, up_weight) + up_bias.astype(wide)
    sigmoid_part = jax.nn.sigmoid(1.702 * hidden)
    active = narrow(hidden * sigmoid_part)
    layer_out = kept + (product(active, down_weight) + down_bias.astype(wide)).reshape(
        frames_here, token_count, model_width
    )
    grad_low = grad_out[0].reshape(frames_here * token_count, model_width)
    grad_rows = grad_low.astype(wide)
    grad_down_weight = product_left_t(active, grad_low)
    grad_down_bias = jnp.sum(grad_rows, 0)
    grad_active = narrow(product_right_t(grad_low, down_weight)).astype(wide)
    grad_hidden = narrow(
        grad_active * (sigmoid_part + 1.702 * hidden * sigmoid_part * (1.0 - sigmoid_part))
    )
    grad_up_weight = product_left_t(mlp_input, grad_hidden)
    grad_up_bias = column_sums(grad_hidden)
    grad_mlp_in = product_right_t(grad_hidden, up_weight).reshape(
        frames_here, token_count, model_width
    )
    grad_gain_two = jnp.sum(grad_mlp_in * normed_two, (0, 1))
    grad_shift_two = jnp.sum(grad_mlp_in, (0, 1))
    grad_kept = grad_rows.reshape(frames_here, token_count, model_width) + norm_back(
        grad_mlp_in, normed_two, inverse_two, gain_two.astype(wide)
    )
    grad_resid = jnp.concatenate(
        [grad_kept, jnp.zeros((frames_here, 1, model_width), wide)], axis=1
    )
    grad_branch = narrow(grad_resid).reshape(frames_here * length, model_width)
    grad_out_weight = product_left_t(mixed_rows, grad_branch)
    grad_out_bias = column_sums(grad_branch)
    grad_mixed = narrow(product_right_t(grad_branch, out_weight)).reshape(head_shape)
    grad_probs = jnp.einsum("fqhd,fkhd->fhqk", grad_mixed, value_rows, preferred_element_type=wide)
    grad_values = narrow(
        jnp.einsum("fhqk,fqhd->fkhd", probs_low, grad_mixed, preferred_element_type=wide)
    )
    grad_scores = narrow(
        attn_probs * (grad_probs - jnp.sum(grad_probs * attn_probs, -1, keepdims=True))
    )
    grad_queries = narrow(
        jnp.einsum("fhqk,fkhd->fqhd", grad_scores, key_rows, preferred_element_type=wide)
        * score_factor
    )
    grad_keys = narrow(
        jnp.einsum("fhqk,fqhd->fkhd", grad_scores, queries, preferred_element_type=wide)
        * score_factor
    )
    flat_shape = (frames_here * length, model_width)
    grad_project = jnp.concatenate(
        [
            grad_queries.reshape(flat_shape),
            grad_keys.reshape(flat_shape),
            grad_values.reshape(flat_shape),
        ],
        axis=1,
    )
    grad_qkv_weight = product_left_t(block_input, grad_project)
    project_sums = column_sums(grad_project)
    grad_qv_bias = jnp.concatenate([project_sums[:model_width], project_sums[2 * model_width :]])
    grad_block_in = product_right_t(grad_project, qkv_weight).reshape(
        frames_here, length, model_width
    )
    grad_gain_one = jnp.sum(grad_block_in * normed_one, (0, 1))
    grad_shift_one = jnp.sum(grad_block_in, (0, 1))
    grad_joined = grad_resid + norm_back(
        grad_block_in, normed_one, inverse_one, gain_one.astype(wide)
    )
    grad_message = grad_joined[:, token_count]
    grad_msg_branch = narrow(grad_message)
    grad_mout_weight = product_left_t(msg_mixed, grad_msg_branch)
    grad_mout_bias = column_sums(grad_msg_branch)
    grad_msg_mixed = narrow(product_right_t(grad_msg_branch, mout_weight)).reshape(
        frames_here, head_count, HEAD_DIM
    )
    grad_msg_probs = jnp.einsum(
        "qhd,khd->hqk", grad_msg_mixed, value_heads, preferred_element_type=wide
    )
    grad_value_all = jnp.einsum(
        "hqk,qhd->khd", msg_probs_low, grad_msg_mixed, preferred_element_type=wide
    ).reshape(frame_total, model_width)
    grad_msg_scores = narrow(
        msg_probs * (grad_msg_probs - jnp.sum(grad_msg_probs * msg_probs, -1, keepdims=True))
    )
    grad_msg_query = narrow(
        jnp.einsum("hqk,khd->qhd", grad_msg_scores, key_heads, preferred_element_type=wide)
        * score_factor
    ).reshape(frames_here, model_width)
    grad_key_all = (
        jnp.einsum("hqk,qhd->khd", grad_msg_scores, query_heads, preferred_element_type=wide)
        * score_factor
    ).reshape(frame_total, model_width)
    grad_key_mine, grad_value_mine = one_scatter((grad_key_all, grad_value_all), "frame", (0, 0))
    grad_msg_project = jnp.concatenate(
        [grad_msg_query, narrow(grad_key_mine), narrow(grad_value_mine)], axis=1
    )
    grad_mqkv_weight = product_left_t(msg_input, grad_msg_project)
    msg_sums = column_sums(grad_msg_project)
    grad_mqv_bias = jnp.concatenate([msg_sums[:model_width], msg_sums[2 * model_width :]])
    grad_msg_in = product_right_t(grad_msg_project, mqkv_weight)
    grad_mnorm_gain = jnp.sum(grad_msg_in * msg_normed, 0)
    grad_mnorm_shift = jnp.sum(grad_msg_in, 0)
    grad_fc = narrow(
        grad_message + norm_back(grad_msg_in, msg_normed, msg_inverse, mnorm_gain.astype(wide))
    )
    grad_fc_weight = product_left_t(class_rows, grad_fc)
    grad_fc_bias = column_sums(grad_fc)
    grad_class = product_right_t(grad_fc, fc_weight)
    grad_tokens = grad_joined[:, :token_count].at[:, 0, :].add(grad_class)
    frame_sums = one_scatter(
        (
            grad_fc_weight,
            grad_fc_bias,
            grad_mnorm_gain,
            grad_mnorm_shift,
            grad_mqkv_weight,
            grad_mqv_bias,
            grad_mout_weight,
            grad_mout_bias,
            grad_gain_one,
            grad_shift_one,
            grad_qkv_weight,
            grad_qv_bias,
            grad_out_weight,
            grad_out_bias,
            grad_gain_two,
            grad_shift_two,
            grad_up_weight,
            grad_up_bias,
            grad_down_weight,
            grad_down_bias,
        ),
        "frame",
        (0, 0, 0, 0, 0, 0, 0, 0, 0, 0, 0, 0, 0, 0, 0, 0, 0, 0, 0, 0),
    )
    reduced = (
        taken_together(frame_sums[0].astype(jnp.bfloat16), "video").astype(jnp.float32),
        taken_together(frame_sums[1].astype(jnp.bfloat16), "video").astype(jnp.float32),
        taken_together(frame_sums[2].astype(jnp.bfloat16), "video").astype(jnp.float32),
        taken_together(frame_sums[3].astype(jnp.bfloat16), "video").astype(jnp.float32),
        taken_together(frame_sums[4].astype(jnp.bfloat16), "video").astype(jnp.float32),
        taken_together(frame_sums[5].astype(jnp.bfloat16), "video").astype(jnp.float32),
        taken_together(frame_sums[6].astype(jnp.bfloat16), "video").astype(jnp.float32),
        taken_together(frame_sums[7].astype(jnp.bfloat16), "video").astype(jnp.float32),
        taken_together(frame_sums[8].astype(jnp.bfloat16), "video").astype(jnp.float32),
        taken_together(frame_sums[9].astype(jnp.bfloat16), "video").astype(jnp.float32),
        taken_together(frame_sums[10].astype(jnp.bfloat16), "video").astype(jnp.float32),
        taken_together(frame_sums[11].astype(jnp.bfloat16), "video").astype(jnp.float32),
        taken_together(frame_sums[12].astype(jnp.bfloat16), "video").astype(jnp.float32),
        taken_together(frame_sums[13].astype(jnp.bfloat16), "video").astype(jnp.float32),
        taken_together(frame_sums[14].astype(jnp.bfloat16), "video").astype(jnp.float32),
        taken_together(frame_sums[15].astype(jnp.bfloat16), "video").astype(jnp.float32),
        taken_together(frame_sums[16].astype(jnp.bfloat16), "video").astype(jnp.float32),
        taken_together(frame_sums[17].astype(jnp.bfloat16), "video").astype(jnp.float32),
        taken_together(frame_sums[18].astype(jnp.bfloat16), "video").astype(jnp.float32),
        taken_together(frame_sums[19].astype(jnp.bfloat16), "video").astype(jnp.float32),
    )
    return (narrow(layer_out)[None], grad_tokens[None]) + tuple(reduced)


def solution(mesh):
    in_specs = (
        P("video", "frame", None, None),
        P("video", "frame"),
        P("video", "frame", None, None),
        P("frame", None),
        P("frame"),
        P("frame"),
        P("frame"),
        P("frame", None),
        P("frame"),
        P("frame", None),
        P("frame"),
        P("frame"),
        P("frame"),
        P("frame", None),
        P("frame"),
        P("frame", None),
        P("frame"),
        P("frame"),
        P("frame"),
        P("frame", None),
        P("frame"),
        P("frame", None),
        P("frame"),
    )
    out_specs = (
        P("video", "frame", None, None),
        P("video", "frame", None, None),
        P("frame", None),
        P("frame"),
        P("frame"),
        P("frame"),
        P("frame", None),
        P("frame"),
        P("frame", None),
        P("frame"),
        P("frame"),
        P("frame"),
        P("frame", None),
        P("frame"),
        P("frame", None),
        P("frame"),
        P("frame"),
        P("frame"),
        P("frame", None),
        P("frame"),
        P("frame", None),
        P("frame"),
    )
    return jax.shard_map(shards, mesh=mesh, in_specs=in_specs, out_specs=out_specs, check_vma=False)
```

profile of v0, /device:TPU:0, one launch (start us, length us, event | category | flops | bytes accessed | tf_op | source)
XLA Modules:
  0.0 1730.1 jit_solution(13116862078748434667)
XLA Ops:
  28.6 333.5 %all-reduce.6 = (bf16[1536]{0:T(1024)(128)(2,1)S(1)}, bf16[1536]{0:T(1024)(128)(2,1)S(1)}, bf16[768]{0:T(1024)(128)(2,1)S(1)}) all-reduce(bf16[1536]{0:T(1024)(128)(2,1)S(1)} %dynamic-update-slice.4, bf16[1536]{0:T(1024)(128)(2,1)S(1)} %dynamic-update-slice.6, ...), channel_id=1, replica_groups=mesh['frame'=64,'video'=2] {'frame'}, use_global_device_ids=true, to_apply=%add.2 | all-reduce | flops 3840 | bytes 15360
  363.5 13.3 all-reduce.3
  378.5 10.1 reshape.693
  395.7 103.8 %all-gather.2 = bf16[64,4,1536]{2,1,0:T(4,128)(2,1)} all-gather(bf16[1,4,1536]{2,1,0:T(4,128)(2,1)S(1)} %maximum_bitcast_fusion), channel_id=1, replica_groups=mesh['frame'=64,'video'=2] {'frame'}, dimensions={0}, use_global_device_ids=true | all-gather | bytes 798720 | tf_op jit(solution)/shard_map/all_gather | solution.py:26
  507.8 9.7 reshape.697
  525.9 6.1 fusion.16
  535.2 3.8 reshape.709
  542.3 3.8 reshape.710
  549.4 3.8 reshape.711
  556.7 9.4 fusion.109
  566.1 4.9 fusion.48
  575.7 10.6 reshape.699
  601.8 10.2 multiply_convert_fusion.1
  612.0 9.5 convert_reduce_fusion
  621.5 5.5 fusion.94
  630.4 5.6 multiply_reduce_fusion.6
  636.2 9.5 fusion.42
  649.2 8.9 fusion.32
  665.3 3.8 reshape.712
  672.6 10.3 multiply_reduce_fusion
  682.9 11.1 multiply_convert_fusion
  700.0 6.7 fusion.45
  723.1 10.2 multiply_reduce_fusion.2
  737.4 5.7 fusion.31
  750.6 9.0 fusion.92
  784.5 7.2 reshape_reshape.24
  795.3 10.1 fusion.111
  805.4 11.6 reshape_reshape.26
  817.1 9.6 fusion.112
  826.7 10.1 reshape_reshape.27
  836.9 82.8 %reduce-scatter.3.cloned.1.call-done = f32[48,128]{1,0:T(8,128)} async-done(((f32[3072,128]{1,0:T(8,128)}), f32[48,128]{1,0:T(8,128)}) %reduce-scatter.3.cloned.1.call-update) | async-done | bytes 24592 | tf_op jit(solution)/shard_map/reduce_scatter | solution.py:42
  924.1 4.1 fusion.91
  940.5 7.5 reshape_reshape.22
  952.9 23.2 %dynamic-update-slice.12 = f32[64,156888]{1,0:T(8,128)} dynamic-update-slice(f32[64,156888]{1,0:T(8,128)} %dynamic-update-slice.11, f32[64,27648]{1,0:T(8,128)} %reshape_reshape.22, s32[]{} %constant.128, s32[]{} %constant.132) | dynamic-update-slice | bytes 14155780
  977.7 12.0 dynamic-update-slice.14
  994.4 23.2 %dynamic-update-slice.18 = f32[64,156888]{1,0:T(8,128)} dynamic-update-slice(f32[64,156888]{1,0:T(8,128)} %dynamic-update-slice.17, f32[64,27648]{1,0:T(8,128)} %reshape_reshape.24, s32[]{} %constant.128, s32[]{} %constant.139) | dynamic-update-slice | bytes 14155780
  1019.2 12.1 dynamic-update-slice.20
  1036.0 28.7 %dynamic-update-slice.24 = f32[64,156888]{1,0:T(8,128)} dynamic-update-slice(f32[64,156888]{1,0:T(8,128)} %dynamic-update-slice.23, f32[64,36864]{1,0:T(8,128)} %reshape_reshape.26, s32[]{} %constant.128, s32[]{} %constant.146) | dynamic-update-slice | bytes 18874372
  1066.2 28.4 %dynamic-update-slice.26 = f32[64,156888]{1,0:T(8,128)} dynamic-update-slice(f32[64,156888]{1,0:T(8,128)} %dynamic-update-slice.25, f32[64,36864]{1,0:T(8,128)} %reshape_reshape.27, s32[]{} %constant.128, s32[]{} %constant.148) | dynamic-update-slice | bytes 18874372
  1096.1 27.6 %pad.7 = f32[64,157696]{1,0:T(8,128)} pad(f32[64,156888]{1,0:T(8,128)} %dynamic-update-slice.27, f32[]{:T(128)} %constant.58.clone.1), padding=0_0x0_808 | pad | bytes 80533504 | tf_op jit(solution)/shard_map/jit(_pad)/pad | solution.py:41
  1123.7 43.3 %reshape.665 = f32[78848,128]{1,0:T(8,128)} reshape(f32[64,157696]{1,0:T(8,128)} %pad.7) | data formatting | bytes 80740352 | tf_op jit(solution)/shard_map/reshape | solution.py:41
  1171.3 392.6 %reduce-scatter.5.cloned.1.call-done = f32[1232,128]{1,0:T(8,128)} async-done(((f32[78848,128]{1,0:T(8,128)}), f32[1232,128]{1,0:T(8,128)}) %reduce-scatter.5.cloned.1.call-update) | async-done | bytes 630800 | tf_op jit(solution)/shard_map/reduce_scatter | solution.py:42
  1667.6 3.6 all-to-all-done
  1683.8 3.6 all-to-all-done.12
  1692.1 3.9 all-to-all-done.4
  1700.8 3.9 all-to-all-done.10
  1709.5 4.1 all-to-all-done.16
  1718.4 3.8 all-to-all-done.18
  (408 shorter events, 336.5 us)
Async XLA Ops:
  7.2 371.3 %all-gather.12.cloned.1.call-start = ((), (), s32[]{:S(2)}) async-start(), calls=%async_computation.25 | async-start | bytes 6656000 | tf_op jit(solution)/shard_map/all_gather | solution.py:16
  11.2 496.5 %all-gather.14.cloned.1.call-start = ((), (), s32[]{:S(2)}) async-start(), calls=%async_computation.26 | async-start | bytes 6656000 | tf_op jit(solution)/shard_map/all_gather | solution.py:16
  15.2 559.0 %all-gather.10.cloned.1.call-start = ((), (), s32[]{:S(2)}) async-start(), calls=%async_computation.22 | async-start | bytes 5591040 | tf_op jit(solution)/shard_map/all_gather | solution.py:16
  17.7 558.0 %all-gather.16.cloned.1.call-start = ((), (), s32[]{:S(2)}) async-start(), calls=%async_computation.27 | async-start | bytes 8253440 | tf_op jit(solution)/shard_map/all_gather | solution.py:16
  21.7 897.9 %reduce-scatter.3.cloned.1.call-start = ((), (), s32[]{:S(2)}) async-start(), calls=%async_computation.23 | async-start | bytes 1597440 | tf_op jit(solution)/shard_map/reduce_scatter | solution.py:42
  25.0 337.2 %copy-start.4 = (bf16[1,4,197,768]{3,1,2,0:T(4,128)(2,1)S(1)}, bf16[1,4,197,768]{3,1,2,0:T(4,128)(2,1)}, u32[]{:S(2)}) copy-start(bf16[1,4,197,768]{3,1,2,0:T(4,128)(2,1)} %param.27) | copy-start | bytes 3631108
  26.5 336.9 %copy-start.56 = (s32[1,4]{1,0:T(1,128)S(1)}, s32[1,4]{1,0:T(1,128)}, u32[]{:S(2)}) copy-start(s32[1,4]{1,0:T(1,128)} %param.26) | copy-start | bytes 52
  378.5 142.9 %copy-start = (f32[4,197,768]{2,0,1:T(4,128)}, f32[4,197,768]{2,0,1:T(4,128)S(1)}, u32[]{:S(2)}) copy-start(f32[4,197,768]{2,0,1:T(4,128)S(1)} %bitcast_convert_fusion.2) | copy-start | bytes 7262212
  391.9 127.2 %copy-start.27 = (f32[768,4]{0,1:T(4,128)}, f32[768,4]{0,1:T(4,128)S(1)}, u32[]{:S(2)}) copy-start(f32[768,4]{0,1:T(4,128)S(1)} %get-tuple-element.104) | copy-start | bytes 36868
  505.3 12.2 copy-start.17
  505.4 12.1 copy-start.38
  505.6 11.9 copy-start.29
  506.3 11.2 copy-start.40
  507.7 11.4 copy-start.42
  556.7 9.4 copy-start.19
  601.8 10.2 copy-start.22
  601.8 19.7 %slice-start = ((s8[6094848]{0:T(1024)(128)(4,1)}), s8[4194304]{0:T(1024)(128)(4,1)S(1)}, s32[]{:S(2)}) async-start(s8[6094848]{0:T(1024)(128)(4,1)} %bitcast.155), calls=%async_computation.28 | async-start | bytes 8388608
  611.9 9.5 slice-start.1
  682.9 11.1 copy-start.9
  737.4 10.4 copy-start.31
  737.4 10.4 copy-start.34
  780.9 782.9 %reduce-scatter.5.cloned.1.call-start = ((), (), s32[]{:S(2)}) async-start(), calls=%async_computation.24 | async-start | bytes 41000960 | tf_op jit(solution)/shard_map/reduce_scatter | solution.py:42
  826.7 93.7 %copy-start.28 = (f32[768,4]{0,1:T(4,128)S(1)}, f32[768,4]{0,1:T(4,128)}, u32[]{:S(2)}) copy-start(f32[768,4]{0,1:T(4,128)} %copy-done.27) | copy-start | bytes 36868
  826.7 93.7 %copy-start.33 = (f32[768]{0:T(1024)S(1)}, f32[768]{0:T(1024)}, u32[]{:S(2)}) copy-start(f32[768]{0:T(1024)} %copy-done.32) | copy-start | bytes 9220
  826.7 93.8 %copy-start.45 = (f32[4]{0:T(128)S(1)}, f32[4]{0:T(128)}, u32[]{:S(2)}) copy-start(f32[4]{0:T(128)} %copy-done.44) | copy-start | bytes 52
  826.7 93.8 %copy-start.49 = (f32[4]{0:T(128)S(1)}, f32[4]{0:T(128)}, u32[]{:S(2)}) copy-start(f32[4]{0:T(128)} %copy-done.48) | copy-start | bytes 52
  836.9 87.2 %copy-start.36 = (f32[768]{0:T(1024)S(1)}, f32[768]{0:T(1024)}, u32[]{:S(2)}) copy-start(f32[768]{0:T(1024)} %copy-done.35) | copy-start | bytes 9220
  1066.2 28.4 %copy-start.37 = (f32[64,12]{1,0:T(8,128)S(1)}, f32[64,12]{1,0:T(8,128)}, u32[]{:S(2)}) copy-start(f32[64,12]{1,0:T(8,128)} %reshape.664) | copy-start | bytes 9220
  1567.2 6.9 all-to-all-start.1
  1574.7 6.9 all-to-all-start.2
  1582.1 6.9 all-to-all-start.3
  1589.5 6.9 all-to-all-start.7
  1596.9 6.9 all-to-all-start.8
  1604.4 6.9 all-to-all-start.9
  1611.8 6.9 all-to-all-start.13
  1619.2 6.9 all-to-all-start.14
  1626.6 6.9 all-to-all-start.15
  1634.1 6.9 all-to-all-start.19
  1641.5 6.9 all-to-all-start.5
  1648.9 6.9 all-to-all-start.11
  1656.3 6.9 all-to-all-start.17
  1663.8 7.4 all-to-all-start
  1671.9 7.3 all-to-all-start.6
  1679.8 7.5 all-to-all-start.12
  1688.1 8.0 all-to-all-start.4
  1696.7 8.0 all-to-all-start.10
  1705.4 8.2 all-to-all-start.16
  1714.3 8.0 all-to-all-start.18
  (40 other events, 157.4 us)
Sparse Core Ops, SparseCore 0:
  11.9 79.2 all-gather.11
  95.1 75.6 all-gather.13
  174.5 73.2 all-gather.9
  251.5 79.5 all-gather.15
  781.1 138.5 reduce-scatter.2
  1167.2 396.5 reduce-scatter.4
where the time goes:
time: 1740 us; the launch traced here: 1730 us
  waiting for transfers between devices  543 us (31%)
  blocking collectives  451 us (26%)
  local copies, waits for them, and re-layouts  431 us (25%)
  matrix products  152 us (9%)
  other arithmetic  70.6 us (4%)
  starting transfers between devices  65.3 us (4%)
  between operations  17.6 us (1%)
    reduce_scatter x2, waiting for transfers between devices, one_scatter(): lax.psum_scatter(lines, axis, tiled=True).reshape(-1)  475 us
    unnamed x2, blocking collectives  347 us
    unnamed x165, local copies, waits for them, and re-layouts  199 us
    all_gather x1, blocking collectives, side_by_side(): result = lax.all_gather(both, axis, axis=dim, tiled=True)  104 us
    all_to_all x20, waiting for transfers between devices, sent_to_all(): lax.all_to_all(jnp.broadcast_to(x[None], (length, *x.shape)), axis, 0, 0,...  67.1 us
    all_to_all x20, starting transfers between devices, sent_to_all(): lax.all_to_all(jnp.broadcast_to(x[None], (length, *x.shape)), axis, 0, 0,...  65.1 us
    another operation x9, local copies, waits for them, and re-layouts, one_scatter(): lines = jnp.concatenate([b.reshape(length, -1) for b in parts], axis=1)  51.5 us
    reshape x2, local copies, waits for them, and re-layouts, one_scatter(): jnp.pad(lines, ((0, 0), (0, span * 128 - lines.shape[1]))).reshape(-1, 128)  45.9 us
  transfers between devices with their start and end apart: 26, of which 22 were waited for; matrix products, arithmetic and copies ran while one was open for 11% of the time, Pallas kernels for 0%

commit v1 on v0

v1 whole, which is shorter than its diff:
```python
import itertools

import jax
import jax.numpy as jnp
from jax import lax
from jax.sharding import PartitionSpec as P

HEAD_DIM = 64


def narrow(value):
    return value.astype(jnp.bfloat16)


def product(left, right):
    return jnp.dot(left, right, preferred_element_type=jnp.float32)


def product_left_t(left, right):
    return lax.dot_general(
        left, right, (((0,), (0,)), ((), ())), preferred_element_type=jnp.float32
    )


def product_right_t(left, right):
    return lax.dot_general(
        left, right, (((1,), (1,)), ((), ())), preferred_element_type=jnp.float32
    )


def norm_parts(value):
    center = value - jnp.mean(value, -1, keepdims=True)
    inverse = lax.rsqrt(jnp.mean(center * center, -1, keepdims=True) + 1e-05)
    return (center * inverse, inverse)


def norm_back(grad_normed, normed, inverse, gain):
    scaled = grad_normed * gain
    return inverse * (
        scaled
        - jnp.mean(scaled, -1, keepdims=True)
        - normed * jnp.mean(scaled * normed, -1, keepdims=True)
    )


def softmax_rows(scores):
    peak = jnp.max(scores, -1, keepdims=True)
    raised = jnp.exp(scores - peak)
    return raised / jnp.sum(raised, -1, keepdims=True)


def column_sums(value):
    return jnp.sum(value.astype(jnp.float32), 0)


def wide_of(value):
    return value.astype(jnp.float32)


def frame_of(x_hi, y, z, core):
    return ((x_hi * 4 + y) * 4 + z) * 2 + core


PLACES = list(itertools.product(range(2), range(4), range(4), range(2), range(2)))


def moves(to):
    return [(frame_of(*p[:4]) * 2 + p[4], frame_of(*to(*p)[:4]) * 2 + to(*p)[4]) for p in PLACES]


TO_CORE = moves(lambda x, y, z, c, v: (x, y, z, 1 - c, v))
TO_VIDEO = moves(lambda x, y, z, c, v: (x, y, z, c, 1 - v))
TO_HALF = moves(lambda x, y, z, c, v: (1 - x, y, z, c, v))
TO_BOTH = moves(lambda x, y, z, c, v: (1 - x, y, z, c, 1 - v))
ALONG_Z = [[frame_of(x, y, z, c) for z in range(4)] for x in range(2) for y in range(4) for c in range(2)]
ALONG_Y = [[frame_of(x, y, z, c) for y in range(4)] for x in range(2) for z in range(4) for c in range(2)]


def sent(x, pairs):
    return lax.ppermute(x, ("frame", "video"), pairs)


def ring_sum(x, groups):
    got = lax.all_to_all(x, "frame", 0, 0, axis_index_groups=groups, tiled=True)
    return narrow(jnp.sum(wide_of(got), 0))


def scattered(grad, z_first):
    place = lax.axis_index("frame")
    core, half = place % 2, place // 32
    r, n = grad.shape[0] // 64, grad.shape[1]
    parts = grad.reshape(2, 4, 4, 2, r, n)
    parts = parts.transpose((3, 2, 1, 0, 4, 5) if z_first else (3, 1, 2, 0, 4, 5))
    give = lax.dynamic_index_in_dim(parts, 1 - core, 0, keepdims=False)
    keep = lax.dynamic_index_in_dim(parts, core, 0, keepdims=False)
    part = narrow(wide_of(keep) + wide_of(sent(give, TO_CORE)))
    part = ring_sum(part, ALONG_Z if z_first else ALONG_Y)
    part = ring_sum(part, ALONG_Y if z_first else ALONG_Z)
    mine = lax.dynamic_index_in_dim(part, half, 0, keepdims=False)
    other = lax.dynamic_index_in_dim(part, 1 - half, 0, keepdims=False)
    return (
        wide_of(mine)
        + wide_of(sent(mine, TO_VIDEO))
        + wide_of(sent(other, TO_HALF))
        + wide_of(sent(other, TO_BOTH))
    )


def to_everyone(x):
    return lax.all_to_all(jnp.broadcast_to(x[None], (64, *x.shape)), "frame", 0, 0, tiled=True)

def shards(
    tokens_in,
    clip_ids,
    grad_out,
    msg_fc_w,
    msg_fc_b,
    msg_norm_gain,
    msg_norm_shift,
    msg_qkv_w,
    msg_qv_b,
    msg_out_w,
    msg_out_b,
    norm1_gain,
    norm1_shift,
    attn_qkv_w,
    attn_qv_b,
    attn_out_w,
    attn_out_b,
    norm2_gain,
    norm2_shift,
    mlp_in_w,
    mlp_in_b,
    mlp_out_w,
    mlp_out_b,
):
    place = lax.axis_index("frame")
    wide = jnp.float32
    model_width = tokens_in.shape[-1]
    head_count = model_width // HEAD_DIM
    frames_here = tokens_in.shape[1]
    token_count = tokens_in.shape[2]
    length = token_count + 1
    score_factor = HEAD_DIM ** (-0.5)
    inputs = tokens_in[0]
    small = jnp.concatenate(
        [
            inputs[:, 0, :].reshape(-1),
            msg_fc_b,
            msg_norm_gain,
            msg_norm_shift,
            msg_out_b,
            norm1_gain,
            norm1_shift,
            attn_out_b,
            norm2_gain,
            norm2_shift,
            mlp_out_b,
            msg_qv_b,
            attn_qv_b,
            mlp_in_b,
            clip_ids[0].astype(jnp.bfloat16),
        ]
    )
    small = jnp.pad(small, (0, 4096 - small.shape[0])).reshape(32, 128)
    small_all = to_everyone(small).reshape(64, 4096)
    msg_weights = lax.all_gather(
        jnp.concatenate([msg_fc_w, msg_qkv_w, msg_out_w], 1), "frame", axis=0, tiled=True
    )
    attn_weights = lax.all_gather(
        jnp.concatenate([attn_qkv_w, attn_out_w], 1), "frame", axis=0, tiled=True
    )
    up_weight = lax.all_gather(mlp_in_w, "frame", axis=0, tiled=True)
    down_weight = lax.all_gather(mlp_out_w, "frame", axis=0, tiled=True)
    class_all = small_all[:, :3072].reshape(256, model_width)
    at = 3072
    vectors = []
    for size in [12] * 10 + [24, 24, 48, 4]:
        vectors.append(small_all[:, at : at + size].reshape(-1))
        at += size
    (
        fc_bias,
        mnorm_gain,
        mnorm_shift,
        mout_bias,
        gain_one,
        shift_one,
        out_bias,
        gain_two,
        shift_two,
        down_bias,
        mqv_bias,
        qv_bias,
        up_bias,
        group_all,
    ) = vectors
    fc_weight, mqkv_weight, mout_weight = jnp.split(msg_weights, [768, 3072], 1)
    qkv_weight, out_weight = jnp.split(attn_weights, [2304], 1)
    message = product(class_all, fc_weight) + fc_bias.astype(wide)
    msg_normed, msg_inverse = norm_parts(message)
    msg_input = narrow(msg_normed * mnorm_gain.astype(wide) + mnorm_shift.astype(wide))
    msg_project = product(msg_input, mqkv_weight)
    msg_query = narrow(msg_project[:, :model_width] + mqv_bias[:model_width].astype(wide))
    msg_key = narrow(msg_project[:, model_width : 2 * model_width])
    msg_value = narrow(msg_project[:, 2 * model_width :] + mqv_bias[model_width:].astype(wide))
    frame_total = class_all.shape[0]
    query_heads = msg_query.reshape(frame_total, head_count, HEAD_DIM)
    key_heads = msg_key.reshape(frame_total, head_count, HEAD_DIM)
    value_heads = msg_value.reshape(frame_total, head_count, HEAD_DIM)
    same_group = (group_all[:, None] == group_all[None, :])[None]
    msg_scores = (
        jnp.einsum("qhd,khd->hqk", query_heads, key_heads, preferred_element_type=wide)
        * score_factor
    )
    msg_scores = jnp.where(same_group, msg_scores, -1000000000.0)
    msg_probs = softmax_rows(msg_scores)
    msg_probs_low = narrow(msg_probs)
    msg_mixed = narrow(
        jnp.einsum("hqk,khd->qhd", msg_probs_low, value_heads, preferred_element_type=wide).reshape(
            frame_total, model_width
        )
    )
    message_all = message + product(msg_mixed, mout_weight) + mout_bias.astype(wide)
    message_token = lax.dynamic_slice_in_dim(message_all, place * frames_here, frames_here)
    joined = jnp.concatenate([inputs.astype(wide), message_token[:, None, :]], axis=1)
    normed_one, inverse_one = norm_parts(joined)
    block_input = narrow(normed_one * gain_one.astype(wide) + shift_one.astype(wide)).reshape(
        frames_here * length, model_width
    )
    project = product(block_input, qkv_weight)
    head_shape = (frames_here, length, head_count, HEAD_DIM)
    queries = narrow(project[:, :model_width] + qv_bias[:model_width].astype(wide)).reshape(
        head_shape
    )
    key_rows = narrow(project[:, model_width : 2 * model_width]).reshape(head_shape)
    value_rows = narrow(project[:, 2 * model_width :] + qv_bias[model_width:].astype(wide)).reshape(
        head_shape
    )
    scores = (
        jnp.einsum("fqhd,fkhd->fhqk", queries, key_rows, preferred_element_type=wide) * score_factor
    )
    attn_probs = softmax_rows(scores)
    probs_low = narrow(attn_probs)
    mixed_rows = narrow(
        jnp.einsum("fhqk,fkhd->fqhd", probs_low, value_rows, preferred_element_type=wide).reshape(
            frames_here * length, model_width
        )
    )
    branch = product(mixed_rows, out_weight) + out_bias.astype(wide)
    residual = joined + branch.reshape(frames_here, length, model_width)
    kept = residual[:, :token_count]
    normed_two, inverse_two = norm_parts(kept)
    mlp_input = narrow(normed_two * gain_two.astype(wide) + shift_two.astype(wide)).reshape(
        frames_here * token_count, model_width
    )
    hidden = product(mlp_input, up_weight) + up_bias.astype(wide)
    sigmoid_part = jax.nn.sigmoid(1.702 * hidden)
    active = narrow(hidden * sigmoid_part)
    layer_out = kept + (product(active, down_weight) + down_bias.astype(wide)).reshape(
        frames_here, token_count, model_width
    )
    grad_low = grad_out[0].reshape(frames_here * token_count, model_width)
    grad_rows = grad_low.astype(wide)
    grad_down_weight = product_left_t(active, grad_low)
    grad_down_bias = jnp.sum(grad_rows, 0)
    grad_active = narrow(product_right_t(grad_low, down_weight)).astype(wide)
    grad_hidden = narrow(
        grad_active * (sigmoid_part + 1.702 * hidden * sigmoid_part * (1.0 - sigmoid_part))
    )
    grad_up_weight = product_left_t(mlp_input, grad_hidden)
    grad_up_bias = column_sums(grad_hidden)
    grad_mlp_in = product_right_t(grad_hidden, up_weight).reshape(
        frames_here, token_count, model_width
    )
    grad_gain_two = jnp.sum(grad_mlp_in * normed_two, (0, 1))
    grad_shift_two = jnp.sum(grad_mlp_in, (0, 1))
    grad_kept = grad_rows.reshape(frames_here, token_count, model_width) + norm_back(
        grad_mlp_in, normed_two, inverse_two, gain_two.astype(wide)
    )
    grad_resid = jnp.concatenate(
        [grad_kept, jnp.zeros((frames_here, 1, model_width), wide)], axis=1
    )
    grad_branch = narrow(grad_resid).reshape(frames_here * length, model_width)
    grad_out_weight = product_left_t(mixed_rows, grad_branch)
    grad_out_bias = column_sums(grad_branch)
    grad_mixed = narrow(product_right_t(grad_branch, out_weight)).reshape(head_shape)
    grad_probs = jnp.einsum("fqhd,fkhd->fhqk", grad_mixed, value_rows, preferred_element_type=wide)
    grad_values = narrow(
        jnp.einsum("fhqk,fqhd->fkhd", probs_low, grad_mixed, preferred_element_type=wide)
    )
    grad_scores = narrow(
        attn_probs * (grad_probs - jnp.sum(grad_probs * attn_probs, -1, keepdims=True))
    )
    grad_queries = narrow(
        jnp.einsum("fhqk,fkhd->fqhd", grad_scores, key_rows, preferred_element_type=wide)
        * score_factor
    )
    grad_keys = narrow(
        jnp.einsum("fhqk,fqhd->fkhd", grad_scores, queries, preferred_element_type=wide)
        * score_factor
    )
    flat_shape = (frames_here * length, model_width)
    grad_project = jnp.concatenate(
        [
            grad_queries.reshape(flat_shape),
            grad_keys.reshape(flat_shape),
            grad_values.reshape(flat_shape),
        ],
        axis=1,
    )
    grad_qkv_weight = product_left_t(block_input, grad_project)
    project_sums = column_sums(grad_project)
    grad_qv_bias = jnp.concatenate([project_sums[:model_width], project_sums[2 * model_width :]])
    grad_block_in = product_right_t(grad_project, qkv_weight).reshape(
        frames_here, length, model_width
    )
    grad_gain_one = jnp.sum(grad_block_in * normed_one, (0, 1))
    grad_shift_one = jnp.sum(grad_block_in, (0, 1))
    grad_joined = grad_resid + norm_back(
        grad_block_in, normed_one, inverse_one, gain_one.astype(wide)
    )
    grad_message = grad_joined[:, token_count]
    grad_message = wide_of(to_everyone(narrow(grad_message))).reshape(frame_total, model_width)
    grad_msg_branch = narrow(grad_message)
    mine = lambda x: lax.dynamic_slice_in_dim(x, place * 12, 12, 1)
    grad_mout_weight = product_left_t(mine(msg_mixed), grad_msg_branch)
    grad_mout_bias = column_sums(grad_msg_branch)
    grad_msg_mixed = narrow(product_right_t(grad_msg_branch, mout_weight)).reshape(
        frame_total, head_count, HEAD_DIM
    )
    grad_msg_probs = jnp.einsum(
        "qhd,khd->hqk", grad_msg_mixed, value_heads, preferred_element_type=wide
    )
    grad_msg_value = narrow(
        jnp.einsum("hqk,qhd->khd", msg_probs_low, grad_msg_mixed, preferred_element_type=wide)
    ).reshape(frame_total, model_width)
    grad_msg_scores = narrow(
        msg_probs * (grad_msg_probs - jnp.sum(grad_msg_probs * msg_probs, -1, keepdims=True))
    )
    grad_msg_query = narrow(
        jnp.einsum("hqk,khd->qhd", grad_msg_scores, key_heads, preferred_element_type=wide)
        * score_factor
    ).reshape(frame_total, model_width)
    grad_msg_key = narrow(
        jnp.einsum("hqk,qhd->khd", grad_msg_scores, query_heads, preferred_element_type=wide)
        * score_factor
    ).reshape(frame_total, model_width)
    grad_msg_project = jnp.concatenate([grad_msg_query, grad_msg_key, grad_msg_value], axis=1)
    grad_mqkv_weight = product_left_t(mine(msg_input), grad_msg_project)
    msg_sums = column_sums(grad_msg_project)
    grad_mqv_bias = jnp.concatenate([msg_sums[:model_width], msg_sums[2 * model_width :]])
    grad_msg_in = product_right_t(grad_msg_project, mqkv_weight)
    grad_mnorm_gain = jnp.sum(grad_msg_in * msg_normed, 0)
    grad_mnorm_shift = jnp.sum(grad_msg_in, 0)
    grad_fc = narrow(
        grad_message + norm_back(grad_msg_in, msg_normed, msg_inverse, mnorm_gain.astype(wide))
    )
    grad_fc_weight = product_left_t(mine(class_all), grad_fc)
    grad_fc_bias = column_sums(grad_fc)
    grad_fc_mine = lax.dynamic_slice_in_dim(grad_fc, place * frames_here, frames_here)
    grad_class = product_right_t(grad_fc_mine, fc_weight)
    grad_tokens = grad_joined[:, :token_count].at[:, 0, :].add(grad_class)
    up_rows = scattered(narrow(grad_up_weight), True)
    down_rows = scattered(narrow(grad_down_weight), False)
    attn_rows = scattered(narrow(jnp.concatenate([grad_qkv_weight, grad_out_weight], 1)), True)
    sums = [
        *(v.reshape(64, -1) for v in (grad_gain_one, grad_shift_one, grad_out_bias)),
        *(v.reshape(64, -1) for v in (grad_gain_two, grad_shift_two, grad_down_bias)),
        *(v.reshape(64, -1) for v in (grad_qv_bias, grad_up_bias)),
    ]
    sums = jnp.pad(jnp.concatenate(sums, 1), ((0, 0), (0, 256 - 144)))
    sums = jnp.sum(lax.all_to_all(sums, "frame", 0, 0, tiled=True), 0)
    own = [
        lax.dynamic_slice_in_dim(v, place * 12, 12)
        for v in (grad_fc_bias, grad_mnorm_gain, grad_mnorm_shift, grad_mout_bias)
    ]
    own.append(lax.dynamic_slice_in_dim(grad_mqv_bias, place * 24, 24))
    vector_sums = jnp.concatenate([sums[:144], *own])
    vector_sums = vector_sums + sent(vector_sums, TO_VIDEO)
    msg_rows = jnp.concatenate([grad_fc_weight, grad_mqkv_weight, grad_mout_weight], 1)
    msg_rows = msg_rows + wide_of(sent(narrow(msg_rows), TO_VIDEO))
    cuts = [12, 24, 36, 48, 60, 72, 96, 144, 156, 168, 180, 192]
    g1, s1, ob, g2, s2, db, qvb, ub, fb, mg, ms, mob, mqvb = jnp.split(vector_sums, cuts)
    return (
        narrow(layer_out)[None],
        grad_tokens[None],
        msg_rows[:, :768],
        fb,
        mg,
        ms,
        msg_rows[:, 768:3072],
        mqvb,
        msg_rows[:, 3072:],
        mob,
        g1,
        s1,
        attn_rows[:, :2304],
        qvb,
        attn_rows[:, 2304:],
        ob,
        g2,
        s2,
        up_rows,
        ub,
        down_rows,
        db,
    )


def solution(mesh):
    in_specs = (
        P("video", "frame", None, None),
        P("video", "frame"),
        P("video", "frame", None, None),
        P("frame", None),
        P("frame"),
        P("frame"),
        P("frame"),
        P("frame", None),
        P("frame"),
        P("frame", None),
        P("frame"),
        P("frame"),
        P("frame"),
        P("frame", None),
        P("frame"),
        P("frame", None),
        P("frame"),
        P("frame"),
        P("frame"),
        P("frame", None),
        P("frame"),
        P("frame", None),
        P("frame"),
    )
    out_specs = (
        P("video", "frame", None, None),
        P("video", "frame", None, None),
        P("frame", None),
        P("frame"),
        P("frame"),
        P("frame"),
        P("frame", None),
        P("frame"),
        P("frame", None),
        P("frame"),
        P("frame"),
        P("frame"),
        P("frame", None),
        P("frame"),
        P("frame", None),
        P("frame"),
        P("frame"),
        P("frame"),
        P("frame", None),
        P("frame"),
        P("frame", None),
        P("frame"),
    )
    return jax.shard_map(shards, mesh=mesh, in_specs=in_specs, out_specs=out_specs, check_vma=False)
```

time: 1740 us -> 785 us (0.45)
  blocking collectives: 451 us -> 0 us
  waiting for transfers between devices: 543 us -> 259 us
  local copies, waits for them, and re-layouts: 431 us -> 186 us
    reduce_scatter x2 -> x0, waiting for transfers between devices: 475 us -> none  [one_scatter(): lax.psum_scatter(lines, axis, tiled=True).reshape(-1)]
    unnamed x2 -> x0, blocking collectives: 347 us -> none
    all_gather x4, waiting for transfers between devices: 0.06 us -> 188 us  [the longest x1 75.4 us: shards(): lax.all_gather(jnp.concatenate([msg_fc_w, msg_qkv_w, msg_out_w], 1), 'fra...]
    unnamed x165 -> x158, local copies, waits for them, and re-layouts: 199 us -> 40.1 us
    all_gather x1 -> x0, blocking collectives: 104 us -> none  [side_by_side(): result = lax.all_gather(both, axis, axis=dim, tiled=True)]
    another operation x9 -> x1, local copies, waits for them, and re-layouts: 51.5 us -> 0.01 us  [shards(): inputs[:, 0, :].reshape(-1)]
    reshape x26 -> x10, local copies, waits for them, and re-layouts: 55.4 us -> 9.7 us  [the longest x1 7.38 us: scattered(): parts = grad.reshape(2, 4, 4, 2, r, n)]
    pad x1 -> x0, local copies, waits for them, and re-layouts: 27.6 us -> none  [one_scatter(): jnp.pad(lines, ((0, 0), (0, span * 128 - lines.shape[1]))).reshape(-1, 128)]
  transfers between devices with their start and end apart: 26 -> 27, of which waited for: 22 -> 12; matrix products, arithmetic and copies ran while one was open for 11% -> 33% of each run, Pallas kernels for 0% -> 0%
where the time goes in v1:
time: 785 us; the launch traced here: 778 us
  waiting for transfers between devices  259 us (33%)
  local copies, waits for them, and re-layouts  186 us (24%)
  matrix products  167 us (21%)
  other arithmetic  80.9 us (10%)
  starting transfers between devices  69.8 us (9%)
  between operations  15.4 us (2%)
    all_gather x1, waiting for transfers between devices, shards(): lax.all_gather(jnp.concatenate([msg_fc_w, msg_qkv_w, msg_out_w], 1), 'fra...  75.4 us
    all_gather x1, waiting for transfers between devices, shards(): up_weight = lax.all_gather(mlp_in_w, 'frame', axis=0, tiled=True)  70.6 us
    all_to_all x6, waiting for transfers between devices, ring_sum(): got = lax.all_to_all(x, 'frame', 0, 0, axis_index_groups=groups, tiled=True)  55.1 us
    all_gather x1, waiting for transfers between devices, shards(): lax.all_gather(jnp.concatenate([attn_qkv_w, attn_out_w], 1), 'frame', axi...  42 us
    unnamed x158, local copies, waits for them, and re-layouts  40.1 us
    dot_general x7, matrix products, product(): return jnp.dot(left, right, preferred_element_type=jnp.float32)  39.4 us
    dot_general x7, matrix products, product_right_t(): lax.dot_general(left, right, (((1,), (1,)), ((), ())), preferred_element_...  38.5 us
    dot_general x7, matrix products, product_left_t(): lax.dot_general(left, right, (((0,), (0,)), ((), ())), preferred_element_...  34.9 us
  transfers between devices with their start and end apart: 27, of which 12 were waited for; matrix products, arithmetic and copies ran while one was open for 33% of the time, Pallas kernels for 0%

profile of v1, /device:TPU:0, one launch (start us, length us, event | category | flops | bytes accessed | tf_op | source)
XLA Modules:
  0.0 777.9 jit_solution(857484565183253790)
XLA Ops:
  12.7 8.8 %concatenate.50 = bf16[3292]{0:T(1024)(128)(2,1)S(1)} concatenate(bf16[3072]{0:T(1024)(128)(2,1)S(1)} %reshape_squeeze.6, bf16[12]{0:T(256)(128)(2,1)} %param.29, bf16[12]{0:T(256)(128)(2,1)} %param.30, bf16[12]{0:T(256)(128)(2,1)} %param.31, bf16[12]{0:T(256)(128)(2,1)} %param.35, bf16[12]{0:T(256)(128)(2,1)} %param.36, bf16[12]{0:T(256)(128)(2,1)} %param.37, ...), dimensions={0} | concatenate | bytes 13168 | tf_op jit(solution)/shard_map/concatenate | solution.py:146
  22.3 11.5 %all-to-all-start = ((bf16[64,32,128]{2,1,0:T(8,128)(2,1)}), bf16[64,32,128]{2,1,0:T(8,128)(2,1)S(1)}, u32[]{:S(2)}, u32[]{:S(2)}) async-start(bf16[64,32,128]{2,1,0:T(8,128)(2,1)} %broadcast_in_dim.27), calls=%async_computation | async-start | bytes 1048576 | tf_op jit(solution)/shard_map/all_to_all | solution.py:110
  38.9 8.4 %all-to-all-done = bf16[64,32,128]{2,1,0:T(8,128)(2,1)S(1)} async-done(((bf16[64,32,128]{2,1,0:T(8,128)(2,1)}), bf16[64,32,128]{2,1,0:T(8,128)(2,1)S(1)}, u32[]{:S(2)}, u32[]{:S(2)}) %all-to-all-start) | async-done | bytes 524320 | tf_op jit(solution)/shard_map/all_to_all | solution.py:110
  50.6 42.0 %all-gather.12.cloned.1.call-done = bf16[64,12,3072]{2,1,0:T(8,128)(2,1)} async-done(((bf16[1,12,3072]{2,1,0:T(8,128)(2,1)}), bf16[64,12,3072]{2,1,0:T(8,128)(2,1)}) %all-gather.12.cloned.1.call-update) | async-done | bytes 4718608 | tf_op jit(solution)/shard_map/all_gather | solution.py:170
  92.6 7.8 reshape.541
  100.3 70.6 %all-gather.14.cloned.1.call-done = bf16[64,12,3072]{2,1,0:T(8,128)(2,1)} async-done(((bf16[1,12,3072]{2,1,0:T(8,128)(2,1)}), bf16[64,12,3072]{2,1,0:T(8,128)(2,1)}) %all-gather.14.cloned.1.call-update) | async-done | bytes 4718608 | tf_op jit(solution)/shard_map/all_gather | solution.py:173
  170.9 7.6 reshape.543
  178.5 75.4 %all-gather.10.cloned.1.call-done = bf16[64,12,3840]{2,1,0:T(8,128)(2,1)} async-done(((bf16[1,12,3840]{2,1,0:T(8,128)(2,1)}), bf16[64,12,3840]{2,1,0:T(8,128)(2,1)}) %all-gather.10.cloned.1.call-update) | async-done | bytes 5898256 | tf_op jit(solution)/shard_map/all_gather | solution.py:167
  253.9 9.6 %reshape.539 = bf16[768,3840]{1,0:T(8,128)(2,1)} reshape(bf16[64,12,3840]{2,1,0:T(8,128)(2,1)} %all-gather.10.cloned.1.call-done) | data formatting | bytes 11796480
  276.9 3.9 fusion.107
  290.6 6.0 fusion.15
  299.5 3.8 reshape.550
  306.7 4.0 reshape.551
  313.9 3.8 reshape.552
  321.0 9.4 %fusion.108 = (f32[4,12,198]{2,1,0:T(8,128)S(1)}, f32[4,12,198,198]{2,3,1,0:T(8,128)}) fusion(bf16[4,198,12,64]{1,3,2,0:T(8,128)(2,1)} %copy.391, bf16[4,198,12,64]{1,3,2,0:T(8,128)(2,1)} %copy.392), kind=kOutput, calls=%fused_computation.234 | convolution fusion | flops 246514944 | bytes 9998208 | tf_op jit(solution)/shard_map/sub | solution.py:48
  330.4 4.9 fusion.48
  337.7 4.4 convolution_add_fusion
  355.3 12.7 %multiply_convert_fusion.2 = (bf16[788,3072]{1,0:T(8,128)(2,1)}, f32[788,3072]{1,0:T(8,128)}) fusion(f32[3072]{0:T(1024)S(1)} %reshape.532, bf16[788,768]{1,0:T(8,128)(2,1)} %reshape.495, bf16[768,3072]{1,0:T(8,128)(2,1)} %reshape.543), kind=kOutput, calls=%fused_computation.7 | convolution fusion | flops 3735195648 | bytes 20465664 | tf_op jit(solution)/shard_map/dot_general | solution.py:16
  368.0 10.1 %convert_reduce_fusion = (f32[3072]{0:T(1024)S(1)}, bf16[788,3072]{1,0:T(8,128)(2,1)S(1)}) fusion(f32[788,3072]{1,0:T(8,128)} %get-tuple-element.109, f32[3072]{0:T(1024)S(1)} %reshape.532, bf16[788,768]{1,0:T(8,128)(2,1)} %reshape_squeeze.7, bf16[3072,768]{1,0:T(8,128)(2,1)} %all-gather.8.cloned.1.call-done), kind=kOutput, calls=%fused_computation.5 | convolution fusion | flops 3754558464 | bytes 20477952 | tf_op jit(solution)/shard_map/dot_general | solution.py:26
  378.1 9.5 %fusion.98 = (f32[768]{0:T(1024)S(1)}, f32[788]{0:T(1024)S(1)}, f32[788,768]{1,0:T(8,128)}) fusion(f32[768]{0:T(1024)S(1)} %reshape.530, bf16[788,3072]{1,0:T(8,128)(2,1)S(1)} %get-tuple-element.116, bf16[768,3072]{1,0:T(8,128)(2,1)} %reshape.543), kind=kOutput, calls=%fused_computation.225 | convolution fusion | flops 3720064512 | bytes 11990096 | tf_op jit(solution)/shard_map/dot_general | solution.py:26
  391.0 5.6 multiply_reduce_fusion.7
  396.9 9.1 %convolution_add_fusion.1 = f32[788,768]{1,0:T(8,128)} fusion(bf16[788,3072]{1,0:T(8,128)(2,1)} %get-tuple-element.108, bf16[3072,768]{1,0:T(8,128)(2,1)} %all-gather.8.cloned.1.call-done, f32[768]{0:T(1024)S(1)} %reshape.533), kind=kOutput, calls=%fused_computation.96 | convolution fusion | flops 3718855680 | bytes 11983872 | tf_op jit(solution)/shard_map/dot_general | solution.py:16
  409.4 8.9 %fusion.31 = (f32[4,197,768]{2,0,1:T(4,128)S(1)}, bf16[1,4,197,768]{3,1,2,0:T(4,128)(2,1)}) fusion(bf16[1,4,197,768]{3,1,2,0:T(4,128)(2,1)} %param.27, f32[4,197,768]{2,1,0:T(8,128)} %reshape.497, f32[4,197]{0,1:T(8,128)S(1)} %broadcast_multiply_fusion.1, f32[4,197]{0,1:T(8,128)S(1)} %copy.401, f32[768]{0:T(1024)S(1)} %reshape.530, ...), kind=kLoop, calls=%fused_computation.72 | loop fusion | flops 6657024 | bytes 12119360 | tf_op jit(solution)/shard_map/add | solution.py:277
  425.1 3.8 reshape.553
  432.4 10.2 %multiply_reduce_fusion = (f32[4,12,198]{2,1,0:T(8,128)S(1)}, f32[4,12,198,198]{2,3,1,0:T(8,128)}) fusion(f32[4,12,198,198]{2,3,1,0:T(8,128)} %get-tuple-element.106, f32[4,12,198]{2,1,0:T(8,128)S(1)} %get-tuple-element.105, bf16[4,198,12,64]{1,3,2,0:T(8,128)(2,1)} %copy.405, bf16[4,198,12,64]{1,3,2,0:T(8,128)(2,1)} %copy.393), kind=kOutput, calls=%fused_computation.3 | convolution fusion | flops 246505248 | bytes 17563392 | tf_op jit(solution)/shard_map/fqhd,fkhd->fhqk/dot_general | solution.py:287
  442.6 11.1 %multiply_convert_fusion = bf16[4,12,198,198]{2,3,1,0:T(8,128)(2,1)} fusion(f32[4,12,198,198]{2,3,1,0:T(8,128)} %get-tuple-element.111, f32[4,12,198]{2,1,0:T(8,128)S(1)} %get-tuple-element.110, f32[4,12,198,198]{2,3,1,0:T(8,128)} %get-tuple-element.106, f32[4,12,198]{2,1,0:T(8,128)S(1)} %get-tuple-element.105), kind=kLoop, calls=%fused_computation.2 | loop fusion | flops 7527168 | bytes 18893952 | tf_op jit(solution)/shard_map/convert_element_type | solution.py:12
  453.7 4.7 fusion.51
  461.4 6.7 fusion.45
  468.1 4.3 copy.453
  477.7 4.3 copy.454
  484.9 4.3 copy.455
  496.2 7.6 fusion.13
  513.8 9.2 %convolution_convert_fusion.3 = bf16[768,3072]{1,0:T(8,128)(2,1)} fusion(bf16[788,768]{1,0:T(8,128)(2,1)S(1)} %copy-done.33, bf16[788,3072]{1,0:T(8,128)(2,1)} %copy-done.65), kind=kOutput, calls=%fused_computation.23 | convolution fusion | flops 3720609792 | bytes 10770432 | tf_op jit(solution)/shard_map/dot_general | solution.py:20
  523.1 9.7 %convolution_convert_fusion.2 = bf16[3072,768]{1,0:T(8,128)(2,1)} fusion(bf16[788,3072]{1,0:T(8,128)(2,1)} %get-tuple-element.108, bf16[788,768]{1,0:T(8,128)(2,1)S(1)} %copy-done.32), kind=kOutput, calls=%fused_computation.22 | convolution fusion | flops 3720609792 | bytes 10770432 | tf_op jit(solution)/shard_map/dot_general | solution.py:20
  534.4 7.5 all-to-all-start.2
  544.3 9.0 %convolution_convert_fusion = bf16[2,4,4,2,12,2304]{5,4,3,2,1,0:T(8,128)(2,1)} fusion(bf16[2,4,4,2,12,792]{5,4,3,2,1,0:T(8,128)(2,1)} %dot_general.137, bf16[792,2304]{1,0:T(8,128)(2,1)} %constant_dynamic-update-slice_fusion), kind=kOutput, calls=%fused_computation.20 | convolution fusion | flops 2804613120 | bytes 8404992 | tf_op jit(solution)/shard_map/dot_general | solution.py:20
  562.9 7.4 reshape.517
  570.3 4.1 dynamic-slice_bitcast_fusion
  574.9 5.8 fusion.30
  586.6 10.7 %all-to-all-start.1 = ((bf16[64,4,768]{2,1,0:T(4,128)(2,1)}), bf16[64,4,768]{2,1,0:T(4,128)(2,1)S(1)}, u32[]{:S(2)}, u32[]{:S(2)}) async-start(bf16[64,4,768]{2,1,0:T(4,128)(2,1)} %broadcast_in_dim.33), calls=%async_computation.1 | async-start | bytes 786432 | tf_op jit(solution)/shard_map/all_to_all | solution.py:110
  597.3 4.2 constant_dynamic-slice_fusion.1
  611.8 5.0 multiply_reduce_fusion.2
  622.8 4.5 all-to-all-start.3
  640.2 16.8 %all-to-all-done.3 = bf16[4,4,2,12,3072]{4,1,3,2,0:T(4,128)(2,1)} async-done(((bf16[4,4,2,12,3072]{4,1,3,2,0:T(4,128)(2,1)}), bf16[4,4,2,12,3072]{4,1,3,2,0:T(4,128)(2,1)}, u32[]{:S(2)}, u32[]{:S(2)}) %all-to-all-start.3) | async-done | bytes 2359328 | tf_op jit(solution)/shard_map/all_to_all | solution.py:84
  657.0 4.9 all-to-all-start.5
  672.4 18.4 %all-to-all-done.5 = bf16[4,4,2,12,3072]{4,1,3,2,0:T(4,128)(2,1)} async-done(((bf16[4,4,2,12,3072]{4,1,3,2,0:T(4,128)(2,1)}), bf16[4,4,2,12,3072]{4,1,3,2,0:T(4,128)(2,1)}, u32[]{:S(2)}, u32[]{:S(2)}) %all-to-all-start.5) | async-done | bytes 2359328 | tf_op jit(solution)/shard_map/all_to_all | solution.py:84
  690.9 4.5 all-to-all-start.7
  708.9 14.5 %all-to-all-done.7 = bf16[4,4,2,48,768]{4,3,1,2,0:T(8,128)(2,1)} async-done(((bf16[4,4,2,48,768]{4,3,1,2,0:T(8,128)(2,1)}), bf16[4,4,2,48,768]{4,3,1,2,0:T(8,128)(2,1)}, u32[]{:S(2)}, u32[]{:S(2)}) %all-to-all-start.7) | async-done | bytes 2359328 | tf_op jit(solution)/shard_map/all_to_all | solution.py:84
  (377 shorter events, 231.2 us)
Async XLA Ops:
  7.2 27.2 %copy-start.7 = (bf16[1,4,197,768]{3,1,2,0:T(4,128)(2,1)S(1)}, bf16[1,4,197,768]{3,1,2,0:T(4,128)(2,1)}, u32[]{:S(2)}) copy-start(bf16[1,4,197,768]{3,1,2,0:T(4,128)(2,1)} %param.27) | copy-start | bytes 3631108
  7.2 85.4 %all-gather.12.cloned.1.call-start = ((), (), s32[]{:S(2)}) async-start(), calls=%async_computation.11 | async-start | bytes 6389760 | tf_op jit(solution)/shard_map/all_gather | solution.py:170
  8.9 162.0 %all-gather.14.cloned.1.call-start = ((), (), s32[]{:S(2)}) async-start(), calls=%async_computation.12 | async-start | bytes 6389760 | tf_op jit(solution)/shard_map/all_gather | solution.py:173
  9.7 244.2 %all-gather.10.cloned.1.call-start = ((), (), s32[]{:S(2)}) async-start(), calls=%async_computation.10 | async-start | bytes 7987200 | tf_op jit(solution)/shard_map/all_gather | solution.py:167
  22.3 24.9 %all-to-all-start = ((bf16[64,32,128]{2,1,0:T(8,128)(2,1)}), bf16[64,32,128]{2,1,0:T(8,128)(2,1)S(1)}, u32[]{:S(2)}, u32[]{:S(2)}) async-start(bf16[64,32,128]{2,1,0:T(8,128)(2,1)} %broadcast_in_dim.27), calls=%async_computation | async-start | bytes 1048576 | tf_op jit(solution)/shard_map/all_to_all | solution.py:110
  33.8 334.2 %all-gather.8.cloned.1.call-start = ((), (), s32[]{:S(2)}) async-start(), calls=%async_computation.9 | async-start | bytes 4792320 | tf_op jit(solution)/shard_map/all_gather | solution.py:174
  38.9 247.1 %copy-start = (f32[4,197,768]{2,0,1:T(4,128)}, f32[4,197,768]{2,0,1:T(4,128)S(1)}, u32[]{:S(2)}) copy-start(f32[4,197,768]{2,0,1:T(4,128)S(1)} %bitcast_convert_fusion) | copy-start | bytes 7262212
  49.5 216.3 %copy-start.49 = (f32[768]{0:T(1024)}, f32[768]{0:T(1024)S(1)}, u32[]{:S(2)}) copy-start(f32[768]{0:T(1024)S(1)} %reshape.520) | copy-start | bytes 9220
  50.1 240.5 %copy-start.55 = (f32[768]{0:T(1024)}, f32[768]{0:T(1024)S(1)}, u32[]{:S(2)}) copy-start(f32[768]{0:T(1024)S(1)} %reshape.526) | copy-start | bytes 9220
  50.2 240.3 %copy-start.47 = (f32[768]{0:T(1024)}, f32[768]{0:T(1024)S(1)}, u32[]{:S(2)}) copy-start(f32[768]{0:T(1024)S(1)} %reshape.525) | copy-start | bytes 9220
  265.5 19.8 %copy-start.12 = (f32[256,768]{1,0:T(8,128)}, f32[256,768]{1,0:T(8,128)S(1)}, u32[]{:S(2)}) copy-start(f32[256,768]{1,0:T(8,128)S(1)} %get-tuple-element.102) | copy-start | bytes 2359300
  285.3 60.3 %copy-start.42 = (f32[4,1,768]{2,0,1:T(4,128)}, f32[4,1,768]{2,0,1:T(4,128)S(1)}, u32[]{:S(2)}) copy-start(f32[4,1,768]{2,0,1:T(4,128)S(1)} %fusion.84) | copy-start | bytes 36868
  321.0 9.4 %copy-start.30 = (bf16[4,198,12,64]{1,3,2,0:T(8,128)(2,1)S(1)}, bf16[4,198,12,64]{1,3,2,0:T(8,128)(2,1)}, u32[]{:S(2)}) copy-start(bf16[4,198,12,64]{1,3,2,0:T(8,128)(2,1)} %copy.393) | copy-start | bytes 3649540
  378.1 9.5 %copy-start.65 = (bf16[788,3072]{1,0:T(8,128)(2,1)}, bf16[788,3072]{1,0:T(8,128)(2,1)S(1)}, u32[]{:S(2)}) copy-start(bf16[788,3072]{1,0:T(8,128)(2,1)S(1)} %get-tuple-element.116) | copy-start | bytes 14524420
  442.6 11.1 %copy-start.18 = (bf16[4,198,12,64]{1,3,2,0:T(8,128)(2,1)S(1)}, bf16[4,198,12,64]{1,3,2,0:T(8,128)(2,1)}, u32[]{:S(2)}) copy-start(bf16[4,198,12,64]{1,3,2,0:T(8,128)(2,1)} %copy.392) | copy-start | bytes 3649540
  513.8 9.3 %copy-start.32 = (bf16[788,768]{1,0:T(8,128)(2,1)S(1)}, bf16[788,768]{1,0:T(8,128)(2,1)}, u32[]{:S(2)}) copy-start(bf16[788,768]{1,0:T(8,128)(2,1)} %reshape_squeeze.7) | copy-start | bytes 3631108
  523.1 10.5 %copy-start.46 = (f32[64,12]{1,0:T(8,128)S(1)}, f32[64,12]{1,0:T(8,128)}, u32[]{:S(2)}) copy-start(f32[64,12]{1,0:T(8,128)} %reshape.515) | copy-start | bytes 9220
  523.1 18.8 %copy-start.21 = (bf16[768,792]{0,1:T(8,128)(2,1)S(1)}, bf16[768,792]{0,1:T(8,128)(2,1)}, u32[]{:S(2)}) copy-start(bf16[768,792]{0,1:T(8,128)(2,1)} %get-tuple-element.56) | copy-start | bytes 3649540
  534.4 51.3 %all-to-all-start.2 = ((f32[64,1,256]{2,1,0:T(1,128)}), f32[64,1,256]{2,1,0:T(1,128)S(1)}, u32[]{:S(2)}, u32[]{:S(2)}) async-start(f32[64,1,256]{2,1,0:T(1,128)} %copy.427), calls=%async_computation.2 | async-start | bytes 131072 | tf_op jit(solution)/shard_map/all_to_all | solution.py:372
  562.8 54.0 %collective-permute-start.2 = (bf16[4,4,2,12,3072]{4,1,3,2,0:T(4,128)(2,1)}, bf16[4,4,2,12,3072]{4,1,3,2,0:T(4,128)(2,1)}, u32[]{:S(2)}, u32[]{:S(2)}) collective-permute-start(bf16[4,4,2,12,3072]{4,1,3,2,0:T(4,128)(2,1)} %copy.429), channel_id=1, source_target_pairs={{0,2},{1,3},{2,0},{3,1},{4,6},{5,7},{6,4},{7,5},{8,10},{9,11},{10,... | collective-permute-start | bytes 7077896 | tf_op jit(solution)/shard_map/ppermute | solution.py:80
  585.3 48.3 %collective-permute-start.6 = (bf16[4,4,2,12,3072]{4,1,3,2,0:T(4,128)(2,1)}, bf16[4,4,2,12,3072]{4,1,3,2,0:T(4,128)(2,1)}, u32[]{:S(2)}, u32[]{:S(2)}) collective-permute-start(bf16[4,4,2,12,3072]{4,1,3,2,0:T(4,128)(2,1)} %copy.434), channel_id=1, source_target_pairs={{0,2},{1,3},{2,0},{3,1},{4,6},{5,7},{6,4},{7,5},{8,10},{9,11},{10,... | collective-permute-start | bytes 7077896 | tf_op jit(solution)/shard_map/ppermute | solution.py:80
  586.6 23.1 %all-to-all-start.1 = ((bf16[64,4,768]{2,1,0:T(4,128)(2,1)}), bf16[64,4,768]{2,1,0:T(4,128)(2,1)S(1)}, u32[]{:S(2)}, u32[]{:S(2)}) async-start(bf16[64,4,768]{2,1,0:T(4,128)(2,1)} %broadcast_in_dim.33), calls=%async_computation.1 | async-start | bytes 786432 | tf_op jit(solution)/shard_map/all_to_all | solution.py:110
  603.1 64.3 %collective-permute-start.10 = (bf16[4,4,2,48,768]{4,3,1,2,0:T(8,128)(2,1)}, bf16[4,4,2,48,768]{4,3,1,2,0:T(8,128)(2,1)}, u32[]{:S(2)}, u32[]{:S(2)}) collective-permute-start(bf16[4,4,2,48,768]{4,3,1,2,0:T(8,128)(2,1)} %bitcast.171), channel_id=1, source_target_pairs={{0,2},{1,3},{2,0},{3,1},{4,6},{5,7},{6,4},{7,5},{8,10},{9,11},{10,... | collective-permute-start | bytes 7077896 | tf_op jit(solution)/shard_map/ppermute | solution.py:80
  622.8 34.3 %all-to-all-start.3 = ((bf16[4,4,2,12,3072]{4,1,3,2,0:T(4,128)(2,1)}), bf16[4,4,2,12,3072]{4,1,3,2,0:T(4,128)(2,1)}, u32[]{:S(2)}, u32[]{:S(2)}) async-start(bf16[4,4,2,12,3072]{4,1,3,2,0:T(4,128)(2,1)} %copy.431), calls=%async_computation.3 | async-start | bytes 4718592 | tf_op jit(solution)/shard_map/all_to_all | solution.py:84
  640.2 23.2 %copy-start.13 = (f32[256,768]{1,0:T(8,128)S(1)}, f32[256,768]{1,0:T(8,128)}, u32[]{:S(2)}) copy-start(f32[256,768]{1,0:T(8,128)} %copy-done.12) | copy-start | bytes 2359300
  640.2 23.2 %copy-start.50 = (f32[768]{0:T(1024)S(1)}, f32[768]{0:T(1024)}, u32[]{:S(2)}) copy-start(f32[768]{0:T(1024)} %copy-done.49) | copy-start | bytes 9220
  640.2 23.2 %copy-start.54 = (f32[256]{0:T(256)S(1)}, f32[256]{0:T(256)}, u32[]{:S(2)}) copy-start(f32[256]{0:T(256)} %copy-done.53) | copy-start | bytes 3076
  640.2 23.2 %copy-start.62 = (f32[256]{0:T(256)S(1)}, f32[256]{0:T(256)}, u32[]{:S(2)}) copy-start(f32[256]{0:T(256)} %copy-done.61) | copy-start | bytes 3076
  657.0 33.9 %all-to-all-start.5 = ((bf16[4,4,2,12,3072]{4,1,3,2,0:T(4,128)(2,1)}), bf16[4,4,2,12,3072]{4,1,3,2,0:T(4,128)(2,1)}, u32[]{:S(2)}, u32[]{:S(2)}) async-start(bf16[4,4,2,12,3072]{4,1,3,2,0:T(4,128)(2,1)} %copy.436), calls=%async_computation.5 | async-start | bytes 4718592 | tf_op jit(solution)/shard_map/all_to_all | solution.py:84
  672.4 23.5 %copy-start.27 = (bf16[12,64,256]{2,1,0:T(8,128)(2,1)S(1)}, bf16[12,64,256]{2,1,0:T(8,128)(2,1)}, u32[]{:S(2)}) copy-start(bf16[12,64,256]{2,1,0:T(8,128)(2,1)} %fusion.54) | copy-start | bytes 1179652
  672.4 23.5 %copy-start.29 = (bf16[12,64,256]{2,1,0:T(8,128)(2,1)S(1)}, bf16[12,64,256]{2,1,0:T(8,128)(2,1)}, u32[]{:S(2)}) copy-start(bf16[12,64,256]{2,1,0:T(8,128)(2,1)} %copy-done.28) | copy-start | bytes 1179652
  672.4 23.5 %copy-start.41 = (bf16[12,64,256]{2,1,0:T(8,128)(2,1)S(1)}, bf16[12,64,256]{2,1,0:T(8,128)(2,1)}, u32[]{:S(2)}) copy-start(bf16[12,64,256]{2,1,0:T(8,128)(2,1)} %convolution_convert_fusion.6) | copy-start | bytes 1179652
  672.4 23.9 %copy-start.63 = (f32[256]{0:T(256)S(1)}, f32[256]{0:T(256)}, u32[]{:S(2)}) copy-start(f32[256]{0:T(256)} %reduce_sum.366) | copy-start | bytes 3076
  690.9 32.5 %all-to-all-start.7 = ((bf16[4,4,2,48,768]{4,3,1,2,0:T(8,128)(2,1)}), bf16[4,4,2,48,768]{4,3,1,2,0:T(8,128)(2,1)}, u32[]{:S(2)}, u32[]{:S(2)}) async-start(bf16[4,4,2,48,768]{4,3,1,2,0:T(8,128)(2,1)} %fusion.8), calls=%async_computation.7 | async-start | bytes 4718592 | tf_op jit(solution)/shard_map/all_to_all | solution.py:84
  696.5 7.9 %collective-permute-start.1 = (f32[216]{0:T(256)S(1)}, f32[216]{0:T(256)S(1)}, u32[]{:S(2)}, u32[]{:S(2)}) collective-permute-start(f32[216]{0:T(256)S(1)} %concatenate.64), channel_id=1, source_target_pairs={{0,1},{1,0},{2,3},{3,2},{4,5},{5,4},{6,7},{7,6},{8,9},{9,8},{10,11... | collective-permute-start | bytes 2600 | tf_op jit(solution)/shard_map/ppermute | solution.py:80
  703.7 35.0 %collective-permute-start = (bf16[12,3840]{1,0:T(8,128)(2,1)S(1)}, bf16[12,3840]{1,0:T(8,128)(2,1)S(1)}, u32[]{:S(2)}, u32[]{:S(2)}) collective-permute-start(bf16[12,3840]{1,0:T(8,128)(2,1)S(1)} %fusion.78), channel_id=1, source_target_pairs={{0,1},{1,0},{2,3},{3,2},{4,5},{5,4},{6,7},{7,6},{8,9},{9,8},{10,11... | collective-permute-start | bytes 276488 | tf_op jit(solution)/shard_map/ppermute | solution.py:80
  723.4 11.9 %all-to-all-start.4 = ((bf16[4,2,12,3072]{3,1,2,0:T(2,128)(2,1)}), bf16[4,2,12,3072]{3,1,2,0:T(2,128)(2,1)S(1)}, u32[]{:S(2)}, u32[]{:S(2)}) async-start(bf16[4,2,12,3072]{3,1,2,0:T(2,128)(2,1)} %copy.433), calls=%async_computation.4 | async-start | bytes 1179648 | tf_op jit(solution)/shard_map/all_to_all | solution.py:84
  735.3 11.9 %all-to-all-start.6 = ((bf16[4,2,12,3072]{3,1,2,0:T(2,128)(2,1)}), bf16[4,2,12,3072]{3,1,2,0:T(2,128)(2,1)S(1)}, u32[]{:S(2)}, u32[]{:S(2)}) async-start(bf16[4,2,12,3072]{3,1,2,0:T(2,128)(2,1)} %copy.438), calls=%async_computation.6 | async-start | bytes 1179648 | tf_op jit(solution)/shard_map/all_to_all | solution.py:84
  747.2 13.0 %all-to-all-start.8 = ((bf16[4,2,48,768]{3,2,1,0:T(8,128)(2,1)}), bf16[4,2,48,768]{3,2,1,0:T(8,128)(2,1)S(1)}, u32[]{:S(2)}, u32[]{:S(2)}) async-start(bf16[4,2,48,768]{3,2,1,0:T(8,128)(2,1)} %copy.442), calls=%async_computation.8 | async-start | bytes 1179648 | tf_op jit(solution)/shard_map/all_to_all | solution.py:84
  751.0 9.3 %collective-permute-start.5 = (bf16[12,3072]{1,0:T(8,128)(2,1)S(1)}, bf16[12,3072]{1,0:T(8,128)(2,1)S(1)}, u32[]{:S(2)}, u32[]{:S(2)}) collective-permute-start(bf16[12,3072]{1,0:T(8,128)(2,1)S(1)} %bitcast.215), channel_id=1, source_target_pairs={{0,65},{1,64},{2,67},{3,66},{4,69},{5,68},{6,71},{7,70},{8,73},{9,... | collective-permute-start | bytes 221192 | tf_op jit(solution)/shard_map/ppermute | solution.py:80
  751.8 9.3 %collective-permute-start.4 = (bf16[12,3072]{1,0:T(8,128)(2,1)S(1)}, bf16[12,3072]{1,0:T(8,128)(2,1)S(1)}, u32[]{:S(2)}, u32[]{:S(2)}) collective-permute-start(bf16[12,3072]{1,0:T(8,128)(2,1)S(1)} %bitcast.216), channel_id=1, source_target_pairs={{0,64},{1,65},{2,66},{3,67},{4,68},{5,69},{6,70},{7,71},{8,72},{9,... | collective-permute-start | bytes 221192 | tf_op jit(solution)/shard_map/ppermute | solution.py:80
  755.9 9.0 %collective-permute-start.9 = (bf16[12,3072]{1,0:T(8,128)(2,1)S(1)}, bf16[12,3072]{1,0:T(8,128)(2,1)S(1)}, u32[]{:S(2)}, u32[]{:S(2)}) collective-permute-start(bf16[12,3072]{1,0:T(8,128)(2,1)S(1)} %bitcast.213), channel_id=1, source_target_pairs={{0,65},{1,64},{2,67},{3,66},{4,69},{5,68},{6,71},{7,70},{8,73},{9,... | collective-permute-start | bytes 221192 | tf_op jit(solution)/shard_map/ppermute | solution.py:80
  756.7 9.3 %collective-permute-start.8 = (bf16[12,3072]{1,0:T(8,128)(2,1)S(1)}, bf16[12,3072]{1,0:T(8,128)(2,1)S(1)}, u32[]{:S(2)}, u32[]{:S(2)}) collective-permute-start(bf16[12,3072]{1,0:T(8,128)(2,1)S(1)} %bitcast.214), channel_id=1, source_target_pairs={{0,64},{1,65},{2,66},{3,67},{4,68},{5,69},{6,70},{7,71},{8,72},{9,... | collective-permute-start | bytes 221192 | tf_op jit(solution)/shard_map/ppermute | solution.py:80
  758.6 5.1 collective-permute-start.3
  760.3 10.1 %collective-permute-start.13 = (bf16[48,768]{1,0:T(8,128)(2,1)S(1)}, bf16[48,768]{1,0:T(8,128)(2,1)S(1)}, u32[]{:S(2)}, u32[]{:S(2)}) collective-permute-start(bf16[48,768]{1,0:T(8,128)(2,1)S(1)} %get-tuple-element.80), channel_id=1, source_target_pairs={{0,65},{1,64},{2,67},{3,66},{4,69},{5,68},{6,71},{7,70},{8,73},{9,... | collective-permute-start | bytes 221192 | tf_op jit(solution)/shard_map/ppermute | solution.py:80
  761.1 9.3 %collective-permute-start.12 = (bf16[48,768]{1,0:T(8,128)(2,1)S(1)}, bf16[48,768]{1,0:T(8,128)(2,1)S(1)}, u32[]{:S(2)}, u32[]{:S(2)}) collective-permute-start(bf16[48,768]{1,0:T(8,128)(2,1)S(1)} %get-tuple-element.80), channel_id=1, source_target_pairs={{0,64},{1,65},{2,66},{3,67},{4,68},{5,69},{6,70},{7,71},{8,72},{9,... | collective-permute-start | bytes 221192 | tf_op jit(solution)/shard_map/ppermute | solution.py:80
  763.8 4.6 collective-permute-start.7
  764.8 5.6 collective-permute-start.11
  (51 other events, 193.5 us)
Sparse Core Ops, SparseCore 0:
  11.8 80.7 all-gather.11
  95.7 75.1 all-gather.13
  174.7 79.1 all-gather.9
  256.9 71.6 all-gather.7

commit v2 on v1

v2 whole, which is shorter than its diff:
```python
import itertools
import jax
import jax.numpy as jnp
from jax import lax
from jax.experimental import pallas as pl
from jax.experimental.pallas import tpu as pltpu
from jax.sharding import PartitionSpec as P

HEAD_DIM = 64
FRAMES = 4
TOK = 197
SPAN = 208
ROWS = FRAMES * SPAN
D = 768
FF = 3072
HEADS = 12
PAIRS = 6
WIDE = jnp.float32
LOW = jnp.bfloat16
SCALE = HEAD_DIM ** (-0.5)
FC_B, MSG_GAIN, MSG_SHIFT, MOUT_B, GAIN1, SHIFT1, OUT_B, GAIN2, SHIFT2, DOWN_B, MQ_B, MV_B, Q_B, V_B, UP_B = range(15)
VECTOR_ROWS = 24


def narrow(x):
    return x.astype(LOW)


def wide_of(x):
    return x.astype(WIDE)


def mm(a, b):
    return lax.dot_general(a, b, (((1,), (0,)), ((), ())), preferred_element_type=WIDE)


def mm_t(a, b):
    return lax.dot_general(a, b, (((1,), (1,)), ((), ())), preferred_element_type=WIDE)


def normed_of(x):
    center = x - jnp.mean(x, -1, keepdims=True)
    inverse = lax.rsqrt(jnp.mean(center * center, -1, keepdims=True) + 1e-05)
    return center * inverse, inverse


def norm_back(grad, normed, inverse, gain):
    scaled = grad * gain
    return inverse * (
        scaled
        - jnp.mean(scaled, -1, keepdims=True)
        - normed * jnp.mean(scaled * normed, -1, keepdims=True)
    )


def own_lanes(x, which):
    lane = lax.broadcasted_iota(jnp.int32, x.shape, 1)
    return jnp.where((lane < HEAD_DIM) == (which == 0), x, jnp.zeros_like(x))


def either(a, b):
    lane = lax.broadcasted_iota(jnp.int32, a.shape, 1)
    return jnp.where(lane < HEAD_DIM, a, b)


def vec(vec_ref, row):
    return vec_ref[row : row + 1, :]


def fill_joined(tok_ref, msg_ref, joined_ref):
    for f in range(FRAMES):
        joined_ref[f * SPAN : f * SPAN + TOK, :] = wide_of(tok_ref[f])
        joined_ref[f * SPAN + TOK : f * SPAN + TOK + 1, :] = msg_ref[f : f + 1, :]
        joined_ref[f * SPAN + TOK + 1 : (f + 1) * SPAN, :] = jnp.zeros((SPAN - TOK - 1, D), WIDE)


def attend_fwd(q, k, vt, valid, mask):
    out = []
    for h in range(2):
        s = mm_t(own_lanes(k, h), q) * SCALE
        s = mask(s)
        peak = jnp.max(s, 0, keepdims=True)
        e = jnp.exp(s - peak)
        total = jnp.sum(e, 0, keepdims=True)
        o = mm(vt[h * HEAD_DIM : (h + 1) * HEAD_DIM], narrow(e)) / total
        out.append((o, peak + jnp.log(total)))
    return out


def attend_bwd(q, k, v, kt, go, lse, dot, mask):
    dqt, dk, dv = [], [], []
    for h in range(2):
        s = mask(mm_t(own_lanes(k, h), q) * SCALE)
        p = jnp.exp(s - lse[h])
        dp = mm_t(own_lanes(v, h), go)
        ds = narrow(p * (dp - dot[h]))
        dv.append(mm(narrow(p), go))
        dk.append(mm(ds, q))
        dqt.append(mm(kt[h * HEAD_DIM : (h + 1) * HEAD_DIM], ds))
    return (
        narrow(jnp.concatenate(dqt, 0) * SCALE),
        narrow(either(*dk) * SCALE),
        narrow(either(*dv)),
    )


def frame_mask(s):
    key = lax.broadcasted_iota(jnp.int32, s.shape, 0)
    return jnp.where(key <= TOK, s, -1e30)


def attn_fwd_kernel(tok_ref, msg_ref, wqkv_ref, wout_ref, vec_ref,
                    qkv_ref, mixed_ref, kept_ref, lse_ref, blk_ref, vt_ref, ot_ref):
    fill_joined(tok_ref, msg_ref, kept_ref)
    for f in range(FRAMES):
        rows = pl.ds(f * SPAN, SPAN)
        normed, _ = normed_of(kept_ref[rows, :])
        blk_ref[rows, :] = narrow(normed * vec(vec_ref, GAIN1) + vec(vec_ref, SHIFT1))
    for n in range(9):
        cols = pl.ds(n * 256, 256)
        y = mm(blk_ref[...], wqkv_ref[:, cols])
        if n < 3:
            y = y + vec_ref[Q_B : Q_B + 1, n * 256 : (n + 1) * 256]
        if n >= 6:
            y = y + vec_ref[V_B : V_B + 1, (n - 6) * 256 : (n - 5) * 256]
        qkv_ref[:, cols] = narrow(y)
    lse_ref[...] = jnp.zeros_like(lse_ref)

    def frame(f, _):
        rows = pl.ds(pl.multiple_of(f * SPAN, SPAN), SPAN)
        vt_ref[...] = qkv_ref[rows, 2 * D :].T
        for p in range(PAIRS):
            q = qkv_ref[rows, p * 128 : (p + 1) * 128]
            k = qkv_ref[rows, D + p * 128 : D + (p + 1) * 128]
            vt = vt_ref[p * 128 : (p + 1) * 128, :]
            for h, (o, l) in enumerate(attend_fwd(q, k, vt, None, frame_mask)):
                at = p * 128 + h * HEAD_DIM
                ot_ref[at : at + HEAD_DIM, :] = narrow(o)
                lse_ref[f, 2 * p + h : 2 * p + h + 1, :] = l
        mixed_ref[rows, :] = ot_ref[...].T
        return 0

    lax.fori_loop(0, FRAMES, frame, 0)
    kept_ref[...] = kept_ref[...] + mm(mixed_ref[...], wout_ref[...]) + vec(vec_ref, OUT_B)


def whole(shape):
    return pl.BlockSpec(shape, lambda *_: (0,) * len(shape))


def shaped(*shape, dtype=LOW):
    return jax.ShapeDtypeStruct(shape, dtype)


def attn_fwd(tok, msg, wqkv, wout, vectors):
    return pl.pallas_call(
        attn_fwd_kernel,
        out_shape=(shaped(ROWS, 3 * D), shaped(ROWS, D), shaped(ROWS, D, dtype=WIDE),
                   shaped(FRAMES, 16, SPAN, dtype=WIDE), shaped(ROWS, D)),
        scratch_shapes=[pltpu.VMEM((D, SPAN), LOW), pltpu.VMEM((D, SPAN), LOW)],
        compiler_params=pltpu.CompilerParams(vmem_limit_bytes=48 << 20),
        name="frame_attention",
    )(tok, msg, wqkv, wout, vectors)


def valid_rows(shape, first=0):
    row = lax.broadcasted_iota(jnp.int32, shape, 0) + first
    return row % SPAN < TOK


CHUNK = 768
CHUNKS = FF // CHUNK


def mlp_kernel(core_ref, kept_ref, gout_ref, up_ref, down_ref, vec_ref, perm_ref,
               lay_ref, gk_ref, dup_keep_ref, dup_give_ref, down_keep_ref, down_give_ref, sums_ref, dub_ref,
               mlp_ref, mlpt_ref, g_ref, acc_ref, dacc_ref):
    j = pl.program_id(0)

    @pl.when(j == 0)
    def _():
        for f in range(FRAMES):
            rows = pl.ds(f * SPAN, SPAN)
            normed, _ = normed_of(kept_ref[rows, :])
            mlp_ref[rows, :] = narrow(normed * vec(vec_ref, GAIN2) + vec(vec_ref, SHIFT2))
            g = jnp.concatenate([wide_of(gout_ref[f]), jnp.zeros((SPAN - TOK, D), WIDE)], 0)
            g_ref[rows, :] = narrow(g)
        mlpt_ref[...] = narrow(mm_t(perm_ref[...], mlp_ref[...]))
        acc_ref[...] = kept_ref[...] + vec(vec_ref, DOWN_B)
        dacc_ref[...] = jnp.zeros_like(dacc_ref)

    mlp = mlp_ref[...]
    g = g_ref[...]
    up = up_ref[...]
    down = down_ref[...]
    hidden = mm(mlp, up) + vec_ref[pl.ds(UP_B + j, 1), :]
    sig = 1.0 / (1.0 + jnp.exp(-1.702 * hidden))
    act = narrow(hidden * sig)
    acc_ref[...] += mm(act, down)
    gact = wide_of(narrow(mm_t(g, down)))
    gh = narrow(gact * (sig + 1.702 * hidden * sig * (1.0 - sig)))
    dub_ref[0] = jnp.broadcast_to(jnp.sum(wide_of(gh), 0, keepdims=True), (8, CHUNK))
    dup = narrow(mm(mlpt_ref[...], gh))
    dup_keep_ref[...] = dup[: D // 2]
    dup_give_ref[...] = dup[D // 2 :]
    dacc_ref[...] += mm_t(gh, up)
    ddown = narrow(lax.dot_general(act, g, (((0,), (0,)), ((), ())), preferred_element_type=WIDE))
    for core in range(2):

        @pl.when(core_ref[0] == core)
        def _():
            for yl in range(2):
                for z in range(4):
                    at = (yl * 4 + z) * 2
                    down_keep_ref[yl, z, 0] = ddown[(at + core) * 48 : (at + core + 1) * 48]
                    down_give_ref[yl, z, 0] = ddown[(at + 1 - core) * 48 : (at + 2 - core) * 48]

    @pl.when(j == CHUNKS - 1)
    def _():
        for f in range(FRAMES):
            lay_ref[f] = narrow(acc_ref[f * SPAN : f * SPAN + TOK, :])
        dg = jnp.zeros((1, D), WIDE)
        dsh = jnp.zeros((1, D), WIDE)
        db = jnp.zeros((1, D), WIDE)
        for f in range(FRAMES):
            rows = pl.ds(f * SPAN, SPAN)
            normed, inverse = normed_of(kept_ref[rows, :])
            gm = dacc_ref[rows, :]
            gw = wide_of(g_ref[rows, :])
            dg += jnp.sum(gm * normed, 0, keepdims=True)
            dsh += jnp.sum(gm, 0, keepdims=True)
            db += jnp.sum(gw, 0, keepdims=True)
            gk = gw + norm_back(gm, normed, inverse, vec(vec_ref, GAIN2))
            gk_ref[rows, :] = jnp.where(valid_rows(gk.shape), gk, 0.0)
        sums_ref[...] = jnp.concatenate([dg, dsh, db, jnp.zeros((5, D), WIDE)], 0)


def mlp(kept, gout, up, down, vectors, perm, core):
    down_spec = pl.BlockSpec((2, 4, 1, 48, D), lambda j: (j % 2, 0, j // 2, 0, 0))
    up_spec = pl.BlockSpec((D // 2, CHUNK), lambda j: (0, j))
    return pl.pallas_call(
        mlp_kernel,
        grid=(CHUNKS,),
        in_specs=[pl.BlockSpec(memory_space=pltpu.SMEM), whole((ROWS, D)), whole((FRAMES, TOK, D)),
                  pl.BlockSpec((D, CHUNK), lambda j: (0, j)),
                  pl.BlockSpec((CHUNK, D), lambda j: (j, 0)),
                  whole((VECTOR_ROWS, D)), whole((D, D))],
        out_specs=[whole((FRAMES, TOK, D)), whole((ROWS, D)),
                   up_spec, up_spec, down_spec, down_spec,
                   whole((8, D)), pl.BlockSpec((1, 8, CHUNK), lambda j: (j, 0, 0))],
        out_shape=(shaped(FRAMES, TOK, D), shaped(ROWS, D, dtype=WIDE), shaped(D // 2, FF), shaped(D // 2, FF),
                   shaped(4, 4, 2, 48, D), shaped(4, 4, 2, 48, D), shaped(8, D, dtype=WIDE), shaped(CHUNKS, 8, CHUNK, dtype=WIDE)),
        scratch_shapes=[pltpu.VMEM((ROWS, D), LOW), pltpu.VMEM((D, ROWS), LOW), pltpu.VMEM((ROWS, D), LOW),
                        pltpu.VMEM((ROWS, D), WIDE), pltpu.VMEM((ROWS, D), WIDE)],
        compiler_params=pltpu.CompilerParams(vmem_limit_bytes=56 << 20),
        name="mlp_both_ways",
    )(core, kept, gout, up, down, vectors, perm)


def head_sums(go, o):
    t = wide_of(go) * wide_of(o)
    high = narrow(t)
    rest = narrow(t - wide_of(high))
    head = lax.broadcasted_iota(jnp.int32, (16, D), 0)
    lane = lax.broadcasted_iota(jnp.int32, (16, D), 1)
    pick = jnp.where((lane // HEAD_DIM) == head, 1.0, 0.0).astype(LOW)
    return mm_t(pick, high) + mm_t(pick, rest)


def attn_bwd_kernel(gk_ref, mixed_ref, qkv_ref, lse_ref, msg_ref, wqkv_ref, wout_ref, vec_ref, perm_ref,
                    dqkv_ref, dout_ref, sums_ref, gmsg_ref,
                    gb_ref, gmix_ref, kt_ref, dqt_ref, rows_ref):
    gb_ref[...] = narrow(gk_ref[...])
    gb = gb_ref[...]
    gmix_ref[...] = narrow(mm_t(gb, wout_ref[...]))
    turned = narrow(mm_t(perm_ref[...], mixed_ref[...]))
    dout_ref[...] = narrow(mm(turned, gb))

    def frame(f, _):
        rows = pl.ds(pl.multiple_of(f * SPAN, SPAN), SPAN)
        kt_ref[...] = qkv_ref[rows, D : 2 * D].T
        dots = head_sums(gmix_ref[rows, :], mixed_ref[rows, :])
        for p in range(PAIRS):
            cols = lambda part: slice(part * D + p * 128, part * D + (p + 1) * 128)
            q, k, v = (qkv_ref[rows, cols(i)] for i in range(3))
            go = gmix_ref[rows, cols(0)]
            lse = [lse_ref[f, 2 * p + h : 2 * p + h + 1, :] for h in range(2)]
            dot = [dots[2 * p + h : 2 * p + h + 1, :] for h in range(2)]
            dqt, dk, dv = attend_bwd(q, k, v, kt_ref[cols(0), :], go, lse, dot, frame_mask)
            dqt_ref[cols(0), :] = dqt
            dqkv_ref[rows, cols(1)] = dk
            dqkv_ref[rows, cols(2)] = dv
        dqkv_ref[rows, :D] = dqt_ref[...].T
        return 0

    lax.fori_loop(0, FRAMES, frame, 0)
    dqb = jnp.zeros((1, D), WIDE)
    dvb = jnp.zeros((1, D), WIDE)
    db = jnp.zeros((1, D), WIDE)
    for f in range(FRAMES):
        rows = pl.ds(f * SPAN, SPAN)
        dqb += jnp.sum(wide_of(dqkv_ref[rows, :D]), 0, keepdims=True)
        dvb += jnp.sum(wide_of(dqkv_ref[rows, 2 * D :]), 0, keepdims=True)
        db += jnp.sum(wide_of(gb_ref[rows, :]), 0, keepdims=True)
        tile = wide_of(dqkv_ref[f * SPAN + 192 : f * SPAN + 208, :])
        rows_ref[f : f + 1, :] = tile[TOK - 192 : TOK - 191, :]
    rows_ref[FRAMES:, :] = jnp.zeros((8 - FRAMES, 3 * D), WIDE)
    sums_ref[...] = jnp.concatenate([db, dqb, dvb, jnp.zeros((5, D), WIDE)], 0)
    back = mm_t(narrow(rows_ref[...]), wqkv_ref[...])
    normed, inverse = normed_of(msg_ref[...])
    gmsg_ref[...] = norm_back(back[:FRAMES], normed, inverse, vec(vec_ref, GAIN1))


def attn_bwd(gk, mixed, qkv, lse, msg, wqkv, wout, vectors, perm):
    return pl.pallas_call(
        attn_bwd_kernel,
        out_shape=(shaped(ROWS, 3 * D), shaped(D, D), shaped(8, D, dtype=WIDE), shaped(FRAMES, D, dtype=WIDE)),
        scratch_shapes=[pltpu.VMEM((ROWS, D), LOW), pltpu.VMEM((ROWS, D), LOW), pltpu.VMEM((D, SPAN), LOW),
                        pltpu.VMEM((D, SPAN), LOW), pltpu.VMEM((8, 3 * D), WIDE)],
        compiler_params=pltpu.CompilerParams(vmem_limit_bytes=56 << 20),
        name="frame_attention_back",
    )(gk, mixed, qkv, lse, msg, wqkv, wout, vectors, perm)


def qkv_weight_kernel(blk_ref, dqkv_ref, perm_ref, out_ref, turned_ref):
    @pl.when(pl.program_id(0) == 0)
    def _():
        turned_ref[...] = narrow(mm_t(perm_ref[...], blk_ref[...]))

    out_ref[...] = narrow(mm(turned_ref[...], dqkv_ref[...]))


def qkv_weight(blk, dqkv, perm):
    return pl.pallas_call(
        qkv_weight_kernel,
        grid=(3,),
        in_specs=[whole((ROWS, D)), pl.BlockSpec((ROWS, D), lambda j: (0, j)), whole((D, D))],
        out_specs=pl.BlockSpec((D, D), lambda j: (0, j)),
        out_shape=shaped(D, 3 * D),
        scratch_shapes=[pltpu.VMEM((D, ROWS), LOW)],
        compiler_params=pltpu.CompilerParams(vmem_limit_bytes=48 << 20),
        name="qkv_weight_gradient",
    )(blk, dqkv, perm)


def tokens_back_kernel(dqkv_ref, wqkv_ref, gk_ref, tok_ref, msg_ref, gcls_ref, vec_ref,
                       out_ref, sums_ref, joined_ref):
    fill_joined(tok_ref, msg_ref, joined_ref)
    dg = jnp.zeros((1, D), WIDE)
    dsh = jnp.zeros((1, D), WIDE)
    joined_ref2 = joined_ref
    back_all = mm_t(dqkv_ref[...], wqkv_ref[...])
    for f in range(FRAMES):
        rows = pl.ds(f * SPAN, SPAN)
        back = back_all[f * SPAN : (f + 1) * SPAN]
        normed, inverse = normed_of(joined_ref2[rows, :])
        dg += jnp.sum(back * normed, 0, keepdims=True)
        dsh += jnp.sum(back, 0, keepdims=True)
        full = gk_ref[rows, :] + norm_back(back, normed, inverse, vec(vec_ref, GAIN1))
        out_ref[f] = full[:TOK]
        out_ref[f, 0:1, :] = full[0:1] + gcls_ref[f : f + 1, :]
    sums_ref[...] = jnp.concatenate([dg, dsh, jnp.zeros((6, D), WIDE)], 0)


def tokens_back(dqkv, wqkv, gk, tok, msg, gcls, vectors):
    return pl.pallas_call(
        tokens_back_kernel,
        out_shape=(shaped(FRAMES, TOK, D, dtype=WIDE), shaped(8, D, dtype=WIDE)),
        scratch_shapes=[pltpu.VMEM((ROWS, D), WIDE)],
        compiler_params=pltpu.CompilerParams(vmem_limit_bytes=56 << 20),
        name="tokens_back",
    )(dqkv, wqkv, gk, tok, msg, gcls, vectors)


ALL = 256


def group_mask(grow_ref, gcol_ref):
    same = gcol_ref[:, 0:1] == grow_ref[0:1, :]

    def mask(s):
        return jnp.where(same, s, -1000000000.0)

    return mask


def msg_fwd_kernel(cls_ref, w_ref, vec_ref, grow_ref, gcol_ref,
                   message_ref, token_ref, min_ref, qkv_ref, mixed_ref, lse_ref, vt_ref, ot_ref):
    message = mm(cls_ref[...], w_ref[:, :D]) + vec(vec_ref, FC_B)
    message_ref[...] = message
    normed, _ = normed_of(message)
    min_ref[...] = narrow(normed * vec(vec_ref, MSG_GAIN) + vec(vec_ref, MSG_SHIFT))
    for n in range(9):
        y = mm(min_ref[...], w_ref[:, D + n * 256 : D + (n + 1) * 256])
        if n < 3:
            y = y + vec_ref[MQ_B : MQ_B + 1, n * 256 : (n + 1) * 256]
        if n >= 6:
            y = y + vec_ref[MV_B : MV_B + 1, (n - 6) * 256 : (n - 5) * 256]
        qkv_ref[:, n * 256 : (n + 1) * 256] = narrow(y)
    vt_ref[...] = qkv_ref[:, 2 * D :].T
    mask = group_mask(grow_ref, gcol_ref)
    lse_ref[...] = jnp.zeros_like(lse_ref)
    for p in range(PAIRS):
        q = qkv_ref[:, p * 128 : (p + 1) * 128]
        k = qkv_ref[:, D + p * 128 : D + (p + 1) * 128]
        vt = vt_ref[p * 128 : (p + 1) * 128, :]
        for h, (o, l) in enumerate(attend_fwd(q, k, vt, None, mask)):
            at = p * 128 + h * HEAD_DIM
            ot_ref[at : at + HEAD_DIM, :] = narrow(o)
            lse_ref[2 * p + h : 2 * p + h + 1, :] = l
    mixed_ref[...] = ot_ref[...].T
    token_ref[...] = message + mm(mixed_ref[...], w_ref[:, 4 * D :]) + vec(vec_ref, MOUT_B)


def msg_fwd(cls, w, vectors, grow, gcol):
    return pl.pallas_call(
        msg_fwd_kernel,
        out_shape=(shaped(ALL, D, dtype=WIDE), shaped(ALL, D, dtype=WIDE), shaped(ALL, D), shaped(ALL, 3 * D),
                   shaped(ALL, D), shaped(16, ALL, dtype=WIDE)),
        scratch_shapes=[pltpu.VMEM((D, ALL), LOW), pltpu.VMEM((D, ALL), LOW)],
        compiler_params=pltpu.CompilerParams(vmem_limit_bytes=48 << 20),
        name="message_forward",
    )(cls, w, vectors, grow, gcol)


def msg_bwd_kernel(gm_ref, cls_ref, message_ref, min_ref, qkv_ref, mixed_ref, lse_ref, w_ref, vec_ref,
                   grow_ref, gcol_ref, pick_ref,
                   gcls_ref, dw_ref, sums_ref,
                   gmix_ref, kt_ref, dqt_ref, dqkv_ref):
    gb = gm_ref[...]
    pick = pick_ref[...]
    turned = lambda x: narrow(mm_t(pick, x))
    gmix_ref[...] = narrow(mm_t(gb, w_ref[:, 4 * D :]))
    dw_ref[:, 4 * D :] = mm(turned(mixed_ref[...]), gb)
    kt_ref[...] = qkv_ref[:, D : 2 * D].T
    mask = group_mask(grow_ref, gcol_ref)
    dots = head_sums(gmix_ref[...], mixed_ref[...])
    for p in range(PAIRS):
        cols = lambda part: slice(part * D + p * 128, part * D + (p + 1) * 128)
        q, k, v = (qkv_ref[:, cols(i)] for i in range(3))
        go = gmix_ref[:, cols(0)]
        lse = [lse_ref[2 * p + h : 2 * p + h + 1, :] for h in range(2)]
        dot = [dots[2 * p + h : 2 * p + h + 1, :] for h in range(2)]
        dqt, dk, dv = attend_bwd(q, k, v, kt_ref[cols(0), :], go, lse, dot, mask)
        dqt_ref[cols(0), :] = dqt
        dqkv_ref[:, cols(1)] = dk
        dqkv_ref[:, cols(2)] = dv
    dqkv_ref[:, :D] = dqt_ref[...].T
    dqkv = dqkv_ref[...]
    dw_ref[:, D : 4 * D] = mm(turned(min_ref[...]), dqkv)
    back = mm_t(dqkv, w_ref[:, D : 4 * D])
    normed, inverse = normed_of(message_ref[...])
    gfc = narrow(wide_of(gb) + norm_back(back, normed, inverse, vec(vec_ref, MSG_GAIN)))
    dw_ref[:, :D] = mm(turned(cls_ref[...]), gfc)
    gcls_ref[...] = mm_t(gfc, w_ref[:, :D])
    col = lambda x: jnp.sum(wide_of(x), 0, keepdims=True)
    sums_ref[...] = jnp.concatenate(
        [col(gfc), col(back * normed), col(back), col(gb), col(dqkv[:, :D]), col(dqkv[:, 2 * D :]),
         jnp.zeros((2, D), WIDE)], 0)


def msg_bwd(gm, cls, message, mins, qkv, mixed, lse, w, vectors, grow, gcol, pick):
    return pl.pallas_call(
        msg_bwd_kernel,
        out_shape=(shaped(ALL, D, dtype=WIDE), shaped(16, 5 * D, dtype=WIDE), shaped(8, D, dtype=WIDE)),
        scratch_shapes=[pltpu.VMEM((ALL, D), LOW), pltpu.VMEM((D, ALL), LOW), pltpu.VMEM((D, ALL), LOW),
                        pltpu.VMEM((ALL, 3 * D), LOW)],
        compiler_params=pltpu.CompilerParams(vmem_limit_bytes=48 << 20),
        name="message_back",
    )(gm, cls, message, mins, qkv, mixed, lse, w, vectors, grow, gcol, pick)


def frame_of(x_hi, y, z, core):
    return ((x_hi * 4 + y) * 4 + z) * 2 + core


PLACES = list(itertools.product(range(2), range(4), range(4), range(2), range(2)))


def moves(to):
    return [(frame_of(*p[:4]) * 2 + p[4], frame_of(*to(*p)[:4]) * 2 + to(*p)[4]) for p in PLACES]


TO_CORE = moves(lambda x, y, z, c, v: (x, y, z, 1 - c, v))
TO_VIDEO = moves(lambda x, y, z, c, v: (x, y, z, c, 1 - v))
TO_HALF = moves(lambda x, y, z, c, v: (1 - x, y, z, c, v))
TO_BOTH = moves(lambda x, y, z, c, v: (1 - x, y, z, c, 1 - v))
TO_Y = [moves(lambda x, y, z, c, v, k=k: (x, (y + k) % 4, z, c, v)) for k in range(4)]
TO_Z = [moves(lambda x, y, z, c, v, k=k: (x, y, (z + k) % 4, c, v)) for k in range(4)]
PLANE = [[frame_of(x, y, z, c) for y in range(4) for z in range(4)] for x in range(2) for c in range(2)]
ATTN_HALF = 1536
MSG_HALF = 1920


def sent(x, pairs):
    return lax.ppermute(x, ("frame", "video"), pairs)


def to_everyone(x):
    return lax.all_to_all(jnp.broadcast_to(x[None], (64, *x.shape)), "frame", 0, 0, tiled=True)


def assemble_kernel(place_ref, *refs):
    pieces, (attn_ref, msg_ref, sems) = refs[:12], refs[12:]
    place = place_ref[0]
    core = lax.rem(place, 2)
    y = lax.rem(lax.div(place, 8), 4)
    x = lax.div(place, 32)
    copies = []

    def copy(src, dst_ref, x_at, y_at, col, width):
        row = pl.multiple_of((x_at * 4 + y_at) * 96, 96)
        dst = dst_ref.at[pl.ds(row, 96), pl.ds(pl.multiple_of(col, 128), width)]
        done = pltpu.make_async_copy(src, dst, sems.at[len(copies)])
        done.start()
        copies.append(done)

    for who in range(2):
        owner = core if who == 0 else 1 - core
        for k in range(4):
            for h in range(2):
                copy(pieces[who * 4 + k].at[h], attn_ref, x if h == 0 else 1 - x,
                     lax.rem(y + 4 - k, 4), owner * ATTN_HALF, ATTN_HALF)
        for h in range(2):
            for k in range(4):
                copy(pieces[8 + who * 2 + h].at[k], msg_ref, x if h == 0 else 1 - x,
                     lax.rem(y + 4 - k, 4), owner * MSG_HALF, MSG_HALF)
    for done in copies:
        done.wait()


def assemble(place, pieces):
    anywhere = pl.BlockSpec(memory_space=pl.ANY)
    return pl.pallas_call(
        assemble_kernel,
        in_specs=[pl.BlockSpec(memory_space=pltpu.SMEM)] + [anywhere] * 12,
        out_specs=(anywhere, anywhere),
        out_shape=(shaped(D, 2 * ATTN_HALF), shaped(D, 2 * MSG_HALF)),
        scratch_shapes=[pltpu.SemaphoreType.DMA((32,))],
        name="assemble_weights",
    )(place, *pieces)


def gathered(place, attn, msg):
    core = place % 2
    z = place // 2 % 4
    cols = lambda w, half, which: lax.dynamic_slice_in_dim(w, which * half, half, 1)
    mine = jnp.concatenate([cols(attn, ATTN_HALF, core), cols(msg, MSG_HALF, core)], 1)
    give = jnp.concatenate([cols(attn, ATTN_HALF, 1 - core), cols(msg, MSG_HALF, 1 - core)], 1)
    got = sent(give, TO_CORE)
    pair = jnp.where(core == 0, jnp.concatenate([mine, got], 0), jnp.concatenate([got, mine], 0))
    ring = [pair, *(sent(pair, TO_Z[k]) for k in range(1, 4))]
    ring = jnp.stack([ring[-t % 4] for t in range(7)])
    slab = lax.dynamic_slice_in_dim(ring, (4 - z) % 4, 4, 0).reshape(96, -1)
    part_a, part_b = slab[:, :ATTN_HALF], slab[:, ATTN_HALF:]
    side_a = jnp.stack([part_a, sent(part_a, TO_HALF)])
    side_b = jnp.stack([part_b, *(sent(part_b, TO_Y[k]) for k in range(1, 4))])
    all_a = [side_a, *(sent(side_a, TO_Y[k]) for k in range(1, 4))]
    all_b = [side_b, sent(side_b, TO_HALF)]
    pieces = [*all_a, *(sent(a, TO_CORE) for a in all_a), *all_b, *(sent(b, TO_CORE) for b in all_b)]
    return assemble(place.reshape(1), pieces)


def row_order(place):
    row = jnp.arange(D, dtype=jnp.int32)
    r, x, z, y, c = row % 12, row // 12 % 2, row // 24 % 4, row // 96 % 4, row // 384
    natural = ((((x * 4 + y) * 4 + z) * 2) + jnp.where(c == 0, place % 2, 1 - place % 2)) * 12 + r
    return (natural[:, None] == row[None, :]).astype(LOW)


def add_pack_kernel(keep_up, got_up, keep_down, got_down, out_ref):
    up = wide_of(keep_up[...]) + wide_of(got_up[...])
    down = wide_of(keep_down[0]) + wide_of(got_down[0])
    for i in range(2):
        out_ref[i, :, :FF] = narrow(up[24 * i : 24 * i + 24])
        slab = jnp.concatenate([down[i, 0], down[i, 1]], 0)
        for q in range(4):
            out_ref[i, :, FF + q * D : FF + (q + 1) * D] = narrow(slab[24 * q : 24 * q + 24])


def add_pack(keep_up, got_up, keep_down, got_down):
    down_spec = pl.BlockSpec((1, 2, 2, 48, D), lambda i: (i // 2, i % 2, 0, 0, 0))
    up_spec = pl.BlockSpec((48, FF), lambda i: (i, 0))
    return pl.pallas_call(
        add_pack_kernel,
        grid=(8,),
        in_specs=[up_spec, up_spec, down_spec, down_spec],
        out_specs=pl.BlockSpec((2, 24, 2 * FF), lambda i: (i, 0, 0)),
        out_shape=shaped(16, 24, 2 * FF),
        compiler_params=pltpu.CompilerParams(vmem_limit_bytes=32 << 20),
        name="add_mlp_gradients",
    )(keep_up, got_up, keep_down, got_down)


def plane_sum(parts):
    got = lax.all_to_all(parts, "frame", 0, 0, axis_index_groups=PLANE, tiled=True)
    return narrow(jnp.sum(wide_of(got), 0))


def last_sum(mine, other):
    return wide_of(mine) + wide_of(sent(mine, TO_VIDEO)) + wide_of(sent(other, TO_HALF)) + wide_of(sent(other, TO_BOTH))


def shards(
    tokens_in,
    clip_ids,
    grad_out,
    msg_fc_w,
    msg_fc_b,
    msg_norm_gain,
    msg_norm_shift,
    msg_qkv_w,
    msg_qv_b,
    msg_out_w,
    msg_out_b,
    norm1_gain,
    norm1_shift,
    attn_qkv_w,
    attn_qv_b,
    attn_out_w,
    attn_out_b,
    norm2_gain,
    norm2_shift,
    mlp_in_w,
    mlp_in_b,
    mlp_out_w,
    mlp_out_b,
):
    place = lax.axis_index("frame").astype(jnp.int32)
    core, half = place % 2, place // 32
    tok = tokens_in[0]
    small = jnp.concatenate(
        [
            tok[:, 0, :].reshape(-1),
            msg_fc_b,
            msg_norm_gain,
            msg_norm_shift,
            msg_out_b,
            norm1_gain,
            norm1_shift,
            attn_out_b,
            norm2_gain,
            norm2_shift,
            mlp_out_b,
            msg_qv_b,
            attn_qv_b,
            mlp_in_b,
            clip_ids[0].astype(LOW),
        ]
    )
    small = jnp.pad(small, (0, 4096 - small.shape[0])).reshape(32, 128)
    small_all = to_everyone(small).reshape(64, 4096)
    up_rows = mlp_in_w.reshape(12, 4, D).transpose(1, 0, 2).reshape(48, D)
    mlp_all = lax.all_gather(jnp.concatenate([up_rows, mlp_out_w], 1), "frame", axis=0, tiled=True)
    w_attn, w_msg = gathered(
        place,
        jnp.concatenate([attn_qkv_w, attn_out_w], 1),
        jnp.concatenate([msg_fc_w, msg_qkv_w, msg_out_w], 1),
    )
    up = mlp_all[:, :D].reshape(64, 4, 12, D).transpose(0, 2, 1, 3).reshape(D, FF)
    down = mlp_all[:, D:]
    cls = small_all[:, :3072].reshape(ALL, D)
    vectors = []
    at = 3072
    for size in [12] * 10 + [24, 24, 48]:
        vectors.append(small_all[:, at : at + size].reshape(-1, D))
        at += size
    vectors = jnp.concatenate(vectors, 0).astype(WIDE)
    vectors = jnp.pad(vectors, ((0, VECTOR_ROWS - vectors.shape[0]), (0, 0)))
    groups = wide_of(small_all[:, at : at + 4].reshape(ALL))
    grow = jnp.broadcast_to(groups[None], (8, ALL))
    gcol = jnp.broadcast_to(groups[:, None], (ALL, 128))
    order = row_order(place)
    pick_row = jnp.arange(16, dtype=jnp.int32)[:, None]
    pick_col = jnp.arange(D, dtype=jnp.int32)[None, :]
    pick = ((pick_row < 12) & (pick_col == place * 12 + pick_row)).astype(LOW)
    w_qkv, w_out = w_attn[:, : 3 * D], w_attn[:, 3 * D :]

    message, token, mins, mqkv, mmixed, mlse = msg_fwd(cls, w_msg, vectors, grow, gcol)
    msg = lax.dynamic_slice_in_dim(token, place * FRAMES, FRAMES)
    qkv, mixed, kept, lse, blk = attn_fwd(tok, msg, w_qkv, w_out, vectors)
    lay, gk, dup_keep, dup_give, down_keep, down_give, sums_mlp, dub = mlp(
        kept, grad_out[0], up, down, vectors, order, core.reshape(1)
    )
    dup_got, down_got = sent(dup_give, TO_CORE), sent(down_give, TO_CORE)
    mlp_sum = plane_sum(add_pack(dup_keep, dup_got, down_keep, down_got))
    dqkv, dout, sums_attn, gmsg = attn_bwd(gk, mixed, qkv, lse, msg, w_qkv, w_out, vectors, order)
    gmsg_all = to_everyone(narrow(gmsg)).reshape(ALL, D)
    dwqkv = qkv_weight(blk, dqkv, order)
    attn_part = jnp.concatenate([dwqkv, dout], 1)
    attn_got = sent(attn_part[384:], TO_CORE)
    attn_sum = narrow(wide_of(attn_part[:384]) + wide_of(attn_got)).reshape(16, 24, FF)
    attn_sum = plane_sum(attn_sum)
    gcls, dw_msg, sums_msg = msg_bwd(gmsg_all, cls, message, mins, mqkv, mmixed, mlse, w_msg, vectors, grow, gcol, pick)
    gcls = lax.dynamic_slice_in_dim(gcls, place * FRAMES, FRAMES)
    grad_tokens, sums_tok = tokens_back(dqkv, w_qkv, gk, tok, msg, gcls, vectors)

    rows = jnp.concatenate([mlp_sum[:, :FF], attn_sum], 1).reshape(2, 12, 2 * FF)
    down_rows = mlp_sum[:, FF:].reshape(24, 4, D).transpose(1, 0, 2).reshape(2, 48, D)
    pick_half = lambda x, which: lax.dynamic_index_in_dim(x, which, 0, keepdims=False)
    rows = last_sum(pick_half(rows, half), pick_half(rows, 1 - half))
    down_rows = last_sum(pick_half(down_rows, half), pick_half(down_rows, 1 - half))
    msg_rows = dw_msg[:12]
    msg_rows = msg_rows + wide_of(sent(narrow(msg_rows), TO_VIDEO))
    sums = jnp.concatenate(
        [sums_tok[:2], sums_attn[:1], sums_mlp[:3]], 0
    ).reshape(6, 64, 12).transpose(1, 0, 2).reshape(64, 72)
    sums = jnp.concatenate(
        [sums, sums_attn[1:3].reshape(64, 24), dub[:, 0].reshape(64, 48), jnp.zeros((64, 112), WIDE)], 1
    )
    sums = jnp.sum(lax.all_to_all(sums, "frame", 0, 0, tiled=True), 0)[:144]
    own = lax.dynamic_slice_in_dim(sums_msg[:4], place * 12, 12, 1).reshape(-1)
    own_qv = lax.dynamic_slice_in_dim(sums_msg[4:6].reshape(-1), place * 24, 24)
    sums = jnp.concatenate([sums, own, own_qv])
    sums = sums + sent(sums, TO_VIDEO)
    cuts = [12, 24, 36, 48, 60, 72, 96, 144, 156, 168, 180, 192]
    g1, s1, ob, g2, s2, db, qvb, ub, fb, mg, ms, mob, mqvb = jnp.split(sums, cuts)
    return (
        lay[None],
        grad_tokens[None],
        msg_rows[:, :D],
        fb,
        mg,
        ms,
        msg_rows[:, D : 4 * D],
        mqvb,
        msg_rows[:, 4 * D :],
        mob,
        g1,
        s1,
        rows[:, FF : FF + 3 * D],
        qvb,
        rows[:, FF + 3 * D :],
        ob,
        g2,
        s2,
        rows[:, :FF],
        ub,
        down_rows,
        db,
    )


def solution(mesh):
    in_specs = (
        P("video", "frame", None, None),
        P("video", "frame"),
        P("video", "frame", None, None),
        P("frame", None),
        P("frame"),
        P("frame"),
        P("frame"),
        P("frame", None),
        P("frame"),
        P("frame", None),
        P("frame"),
        P("frame"),
        P("frame"),
        P("frame", None),
        P("frame"),
        P("frame", None),
        P("frame"),
        P("frame"),
        P("frame"),
        P("frame", None),
        P("frame"),
        P("frame", None),
        P("frame"),
    )
    out_specs = (
        P("video", "frame", None, None),
        P("video", "frame", None, None),
        P("frame", None),
        P("frame"),
        P("frame"),
        P("frame"),
        P("frame", None),
        P("frame"),
        P("frame", None),
        P("frame"),
        P("frame"),
        P("frame"),
        P("frame", None),
        P("frame"),
        P("frame", None),
        P("frame"),
        P("frame"),
        P("frame"),
        P("frame", None),
        P("frame"),
        P("frame", None),
        P("frame"),
    )
    return jax.shard_map(shards, mesh=mesh, in_specs=in_specs, out_specs=out_specs, check_vma=False)
```

time: 785 us -> 856 us (1.090)
  Pallas kernels: 0 us -> 448 us
  matrix products: 167 us -> 0 us
  local copies, waits for them, and re-layouts: 186 us -> 96.1 us
  other arithmetic: 80.9 us -> 21 us
  waiting for transfers between devices: 259 us -> 201 us
    pallas_call x0 -> x9, Pallas kernels: none -> 448 us  [the longest x1 323 us: assemble(): pl.pallas_call(assemble_kernel, in_specs=[pl.BlockSpec(memory_space=pltpu...]
    all_gather x4 -> x1, waiting for transfers between devices: 188 us -> 0.01 us  [shards(): lax.all_gather(jnp.concatenate([up_rows, mlp_out_w], 1), 'frame', axis=0,...]
    dot_general x31 -> x0, matrix products: 154 us -> none  [the longest x7 39.4 us: product(): return jnp.dot(left, right, preferred_element_type=jnp.float32)]
    ppermute x14 -> x29, waiting for transfers between devices: 3.18 us -> 104 us  [sent(): return lax.ppermute(x, ('frame', 'video'), pairs)]
    reshape x31 -> x27, local copies, waits for them, and re-layouts: 78.5 us -> 19.6 us  [the longest x1 8.72 us: shards(): mlp_all[:, :D].reshape(64, 4, 12, D).transpose(0, 2, 1, 3).reshape(D, FF)]
    all_to_all x7 -> x3, waiting for transfers between devices: 55.1 us -> 84.3 us  [the longest x2 78.8 us: plane_sum(): lax.all_to_all(parts, 'frame', 0, 0, axis_index_groups=PLANE, tiled=True)]
    convert_element_type x15 -> x6, other arithmetic: 30.9 us -> 7.37 us  [the longest x2 4.61 us: narrow(): return x.astype(LOW)]
    reduce_sum x20 -> x3, other arithmetic: 29.8 us -> 6.35 us  [the longest x2 5.22 us: plane_sum(): return narrow(jnp.sum(wide_of(got), 0))]
  transfers between devices with their start and end apart: 27 -> 35, of which waited for: 12 -> 16; matrix products, arithmetic and copies ran while one was open for 33% -> 7% of each run, Pallas kernels for 0% -> 44%
where the time goes in v2:
time: 856 us; the launch traced here: 845 us
  Pallas kernels  448 us (52%)
  waiting for transfers between devices  201 us (23%)
  local copies, waits for them, and re-layouts  96.1 us (11%)
  starting transfers between devices  63.6 us (7%)
  other arithmetic  21 us (2%)
  between operations  15.6 us (2%)
    pallas_call x1, Pallas kernels, assemble(): pl.pallas_call(assemble_kernel, in_specs=[pl.BlockSpec(memory_space=pltpu...  323 us
    ppermute x29, waiting for transfers between devices, sent(): return lax.ppermute(x, ('frame', 'video'), pairs)  104 us
    all_to_all x2, waiting for transfers between devices, plane_sum(): lax.all_to_all(parts, 'frame', 0, 0, axis_index_groups=PLANE, tiled=True)  78.8 us
    pallas_call x1, Pallas kernels, mlp(): pl.pallas_call(mlp_kernel, grid=(CHUNKS,), in_specs=[pl.BlockSpec(memory_...  40.3 us
    unnamed x127, local copies, waits for them, and re-layouts  35.9 us
    ppermute x29, starting transfers between devices, sent(): return lax.ppermute(x, ('frame', 'video'), pairs)  34 us
    pallas_call x1, Pallas kernels, attn_bwd(): pl.pallas_call(attn_bwd_kernel, out_shape=(shaped(ROWS, 3 * D), shaped(D,...  24.7 us
    pallas_call x1, Pallas kernels, attn_fwd(): pl.pallas_call(attn_fwd_kernel, out_shape=(shaped(ROWS, 3 * D), shaped(RO...  19.8 us
  transfers between devices with their start and end apart: 35, of which 16 were waited for; matrix products, arithmetic and copies ran while one was open for 7% of the time, Pallas kernels for 44%

profile of v2, /device:TPU:0, one launch (start us, length us, event | category | flops | bytes accessed | tf_op | source)
XLA Modules:
  0.0 845.0 jit_solution(18174318545505635126)
XLA Ops:
  15.4 4.2 collective-permute-start.1
  20.9 6.5 collective-permute-done.1
  28.2 2.7 collective-permute-done.3
  32.8 2.9 collective-permute-start.13
  37.1 6.1 collective-permute-done.12
  43.2 9.1 %collective-permute-done.13 = bf16[96,1920]{1,0:T(8,128)(2,1)S(1)} collective-permute-done((bf16[96,1920]{1,0:T(8,128)(2,1)S(1)}, bf16[96,1920]{1,0:T(8,128)(2,1)S(1)}, u32[]{:S(2)}, u32[]{:S(2)}) %collective-permute-start.13) | collective-permute-done | bytes 368672 | tf_op jit(solution)/shard_map/ppermute | solution.py:496
  52.7 3.0 collective-permute-start.15
  56.4 57.0 %collective-permute-done.4 = bf16[96,1536]{1,0:T(8,128)(2,1)S(1)} collective-permute-done((bf16[96,1536]{1,0:T(8,128)(2,1)S(1)}, bf16[96,1536]{1,0:T(8,128)(2,1)S(1)}, u32[]{:S(2)}, u32[]{:S(2)}) %collective-permute-start.4) | collective-permute-done | bytes 294944 | tf_op jit(solution)/shard_map/ppermute | solution.py:496
  114.3 3.0 collective-permute-start.6
  120.5 15.3 %collective-permute-done.6.refs_2_ = bf16[2,96,1536]{2,1,0:T(8,128)(2,1)} collective-permute-done((bf16[2,96,1536]{2,1,0:T(8,128)(2,1)}, bf16[2,96,1536]{2,1,0:T(8,128)(2,1)}, u32[]{:S(2)}, u32[]{:S(2)}) %collective-permute-start.6) | collective-permute-done | bytes 589856 | tf_op jit(solution)/shard_map/ppermute | solution.py:496
  136.7 6.3 all-to-all-start
  143.0 2.4 copy.83
  146.7 9.5 %all-to-all-done = bf16[64,32,128]{2,1,0:T(8,128)(2,1)} async-done(((bf16[64,32,128]{2,1,0:T(8,128)(2,1)}), bf16[64,32,128]{2,1,0:T(8,128)(2,1)}, u32[]{:S(2)}, u32[]{:S(2)}) %all-to-all-start) | async-done | bytes 524320 | tf_op jit(solution)/shard_map/all_to_all | solution.py:500
  164.5 323.0 %assemble_weights.1 = (bf16[768,3072]{1,0:T(8,128)(2,1)}, bf16[768,3840]{1,0:T(8,128)(2,1)}) custom-call(s32[1]{0:T(128)} %bitcast.4.place_ref, bf16[2,96,1536]{2,1,0:T(8,128)(2,1)} %pad_maximum_fusion.2.refs_0_, bf16[2,96,1536]{2,1,0:T(8,128)(2,1)} %collective-permute-done.5.refs_1_, bf16[2,96,1536]{2,1,0:T(8,128)(2,1)} %collective-permute-done.6.refs_2_, ...), custom_call_target="tpu_custom_call" | custom-call | tf_op jit(solution)/shard_map/assemble_weights/pallas_call | solution.py:534
  487.5 4.0 slice.141.wqkv_ref
  493.0 8.6 %message_forward.1 = (f32[256,768]{1,0:T(8,128)S(1)}, f32[256,768]{1,0:T(8,128)S(1)}, bf16[256,768]{1,0:T(8,128)(2,1)S(1)}, bf16[256,2304]{1,0:T(8,128)(2,1)S(1)...) custom-call(bf16[256,768]{1,0:T(8,128)(2,1)S(1)} %reshape.309.cls_ref, bf16[768,3840]{1,0:T(8,128)(2,1)} %get-tuple-element.52.w_ref, ...), custom_call_target="tpu_custom_call" | custom-call | tf_op jit(solution)/shard_map/message_forward/pallas_call | solution.py:416
  505.7 19.8 %frame_attention.1 = (bf16[832,2304]{1,0:T(8,128)(2,1)}, bf16[832,768]{1,0:T(8,128)(2,1)S(1)}, f32[832,768]{1,0:T(8,128)}, f32[4,16,208]{2,1,0:T(8,128)S(1)}, bf16[832,768]{1,0:T(8,128)(2,1)S(1)}) custom-call(bf16[4,197,768]{2,1,0:T(8,128)(2,1)S(1)} %bitcast.61, f32[4,768]{1,0:T(4,128)S(1)} %constant_dynamic-slice_fusion.2.msg_ref, ...), custom_call_target="tpu_custom_call" | custom-call | tf_op jit(solution)/shard_map/frame_attention/pallas_call | solution.py:156
  527.5 8.0 fusion.29
  535.6 8.7 %reshape.327 = bf16[64,4,12,768]{3,2,1,0:T(8,128)(2,1)} reshape(bf16[3072,768]{1,0:T(8,128)(2,1)} %get-tuple-element.171) | data formatting | bytes 9437184 | tf_op jit(solution)/shard_map/reshape | solution.py:660
  544.3 5.2 copy.71
  549.5 3.3 copy.78
  552.8 40.3 %mlp_both_ways.1 = (bf16[4,197,768]{2,1,0:T(8,128)(2,1)}, f32[832,768]{1,0:T(8,128)}, bf16[384,3072]{1,0:T(8,128)(2,1)}, bf16[384,3072]{1,0:T(8,128)(2,1)}, bf16...) custom-call(s32[1]{0:T(128)} %bitcast.core_ref, ...), custom_call_target="tpu_custom_call" | custom-call | tf_op jit(solution)/shard_map/mlp_both_ways/pallas_call | solution.py:241
  593.1 24.7 %frame_attention_back.1 = (bf16[832,2304]{1,0:T(8,128)(2,1)}, bf16[768,768]{1,0:T(8,128)(2,1)}, f32[8,768]{1,0:T(8,128)}, f32[4,768]{1,0:T(4,128)}) custom-call(f32[832,768]{1,0:T(8,128)} %get-tuple-element.57.gk_ref, bf16[832,768]{1,0:T(8,128)(2,1)} %copy-done.13, bf16[832,2304]{1,0:T(8,128)(2,1)} %get-tuple-element.59.qkv_ref, f32[4,16,208]{2,1,0:T(8,128)} %copy-done.30, ...), custom_call_target="tpu_custom_call" | custom-call | tf_op jit(solution)/shard_map/frame_attention_back/pallas_call | solution.py:315
  617.8 7.2 qkv_weight_gradient.1
  625.1 1.7 pad_maximum_fusion
  628.6 5.5 all-to-all-start.1
  643.1 3.2 all-to-all-done.1
  646.2 1.8 reshape.329.gm_ref
  657.7 9.0 %message_back.1 = (f32[256,768]{1,0:T(8,128)S(1)}, f32[16,3840]{1,0:T(8,128)S(1)}, f32[8,768]{1,0:T(8,128)S(1)}) custom-call(bf16[256,768]{1,0:T(8,128)(2,1)S(1)} %copy-done.10, bf16[256,768]{1,0:T(8,128)(2,1)S(1)} %copy-done.7, f32[256,768]{1,0:T(8,128)S(1)} %copy-done.19, bf16[256,768]{1,0:T(8,128)(2,1)S(1)} %copy-done.23, ...), custom_call_target="tpu_custom_call" | custom-call | tf_op jit(solution)/shard_map/message_back/pallas_call | solution.py:463
  668.7 10.0 %tokens_back.1 = (f32[4,197,768]{2,1,0:T(8,128)}, f32[8,768]{1,0:T(8,128)}) custom-call(bf16[832,2304]{1,0:T(8,128)(2,1)} %get-tuple-element.61.dqkv_ref, bf16[768,2304]{1,0:T(8,128)(2,1)} %slice.141.wqkv_ref, f32[832,768]{1,0:T(8,128)} %get-tuple-element.57.gk_ref, bf16[4,197,768]{2,1,0:T(8,128)(2,1)} %bitcast.62, f32[4,768]{1,0:T(4,128)} %copy-done.26, ...), custom_call_target="tpu_custom_call" | custom-call | tf_op jit(solution)/shard_map/tokens_back/pallas_call | solution.py:366
  681.6 1.7 copy.72
  687.8 7.4 all-to-all-start.2
  695.2 3.9 add_convert_fusion
  699.1 5.6 all-to-all-done.2
  704.7 4.6 all-to-all-start.4
  711.0 5.1 add_mlp_gradients.1
  716.1 2.2 copy-done.1
  718.3 24.6 %all-to-all-done.4 = bf16[16,24,3072]{2,1,0:T(8,128)(2,1)} async-done(((bf16[16,24,3072]{2,1,0:T(8,128)(2,1)}), bf16[16,24,3072]{2,1,0:T(8,128)(2,1)}, u32[]{:S(2)}, u32[]{:S(2)}) %all-to-all-start.4) | async-done | bytes 2359328 | tf_op jit(solution)/shard_map/all_to_all | solution.py:596
  742.9 5.9 all-to-all-start.3
  750.3 1.7 collective-permute-start.19
  752.0 2.8 copy.75
  755.5 2.4 copy.76
  761.1 2.1 reduce_sum.35
  763.1 54.2 %all-to-all-done.3 = bf16[16,24,6144]{2,1,0:T(8,128)(2,1)} async-done(((bf16[16,24,6144]{2,1,0:T(8,128)(2,1)}), bf16[16,24,6144]{2,1,0:T(8,128)(2,1)}, u32[]{:S(2)}, u32[]{:S(2)}) %all-to-all-start.3) | async-done | bytes 4718624 | tf_op jit(solution)/shard_map/all_to_all | solution.py:596
  817.3 3.2 reduce_sum.34
  820.7 4.1 collective-permute-start.28
  826.5 3.3 collective-permute-start.25
  830.7 4.9 collective-permute-done.23
  (271 shorter events, 77.9 us)
Async XLA Ops:
  7.2 520.3 %all-gather.2.cloned.1.call-start = ((), (), s32[]{:S(2)}) async-start(), calls=%async_computation.5 | async-start | bytes 9584640 | tf_op jit(solution)/shard_map/all_gather | solution.py:654
  13.9 1.4 collective-permute-start
  15.4 12.1 %collective-permute-start.1 = (bf16[24,3456]{1,0:T(8,128)(2,1)S(1)}, bf16[24,3456]{1,0:T(8,128)(2,1)S(1)}, u32[]{:S(2)}, u32[]{:S(2)}) collective-permute-start(bf16[24,3456]{1,0:T(8,128)(2,1)S(1)} %maximum_select_fusion.1), channel_id=1, source_target_pairs={{0,12},{1,13},{2,14},{3,15},{4,0},{5,1},{6,2},{7,3},{8,4},{9,5},{1... | collective-permute-start | bytes 497672 | tf_op jit(solution)/shard_map/ppermute | solution.py:496
  19.6 8.6 %collective-permute-start.2 = (bf16[24,3456]{1,0:T(8,128)(2,1)S(1)}, bf16[24,3456]{1,0:T(8,128)(2,1)S(1)}, u32[]{:S(2)}, u32[]{:S(2)}) collective-permute-start(bf16[24,3456]{1,0:T(8,128)(2,1)S(1)} %maximum_select_fusion.1), channel_id=1, source_target_pairs={{0,8},{1,9},{2,10},{3,11},{4,12},{5,13},{6,14},{7,15},{8,0},{9,1},... | collective-permute-start | bytes 497672 | tf_op jit(solution)/shard_map/ppermute | solution.py:496
  19.6 11.3 %collective-permute-start.3 = (bf16[24,3456]{1,0:T(8,128)(2,1)S(1)}, bf16[24,3456]{1,0:T(8,128)(2,1)S(1)}, u32[]{:S(2)}, u32[]{:S(2)}) collective-permute-start(bf16[24,3456]{1,0:T(8,128)(2,1)S(1)} %maximum_select_fusion.1), channel_id=1, source_target_pairs={{0,4},{1,5},{2,6},{3,7},{4,8},{5,9},{6,10},{7,11},{8,12},{9,13},{1... | collective-permute-start | bytes 497672 | tf_op jit(solution)/shard_map/ppermute | solution.py:496
  31.2 12.0 %collective-permute-start.12 = (bf16[96,1920]{1,0:T(8,128)(2,1)S(1)}, bf16[96,1920]{1,0:T(8,128)(2,1)S(1)}, u32[]{:S(2)}, u32[]{:S(2)}) collective-permute-start(bf16[96,1920]{1,0:T(8,128)(2,1)S(1)} %get-tuple-element.173), channel_id=1, source_target_pairs={{0,16},{1,17},{2,18},{3,19},{4,20},{5,21},{6,22},{7,23},{8,24},{9,... | collective-permute-start | bytes 1105928 | tf_op jit(solution)/shard_map/ppermute | solution.py:496
  32.8 19.4 %collective-permute-start.13 = (bf16[96,1920]{1,0:T(8,128)(2,1)S(1)}, bf16[96,1920]{1,0:T(8,128)(2,1)S(1)}, u32[]{:S(2)}, u32[]{:S(2)}) collective-permute-start(bf16[96,1920]{1,0:T(8,128)(2,1)S(1)} %get-tuple-element.173), channel_id=1, source_target_pairs={{0,32},{1,33},{2,34},{3,35},{4,36},{5,37},{6,38},{7,39},{8,40},{9,... | collective-permute-start | bytes 1105928 | tf_op jit(solution)/shard_map/ppermute | solution.py:496
  35.7 16.5 %collective-permute-start.14 = (bf16[96,1920]{1,0:T(8,128)(2,1)S(1)}, bf16[96,1920]{1,0:T(8,128)(2,1)S(1)}, u32[]{:S(2)}, u32[]{:S(2)}) collective-permute-start(bf16[96,1920]{1,0:T(8,128)(2,1)S(1)} %get-tuple-element.173), channel_id=1, source_target_pairs={{0,48},{1,49},{2,50},{3,51},{4,52},{5,53},{6,54},{7,55},{8,56},{9,... | collective-permute-start | bytes 1105928 | tf_op jit(solution)/shard_map/ppermute | solution.py:496
  52.5 84.2 %copy-start.35 = (bf16[4,96,1920]{2,1,0:T(8,128)(2,1)}, bf16[4,96,1920]{2,1,0:T(8,128)(2,1)S(1)}, u32[]{:S(2)}) copy-start(bf16[4,96,1920]{2,1,0:T(8,128)(2,1)S(1)} %pad_maximum_fusion.1.refs_8_) | copy-start | bytes 4423684
  52.5 65.6 %copy-start.43 = (bf16[12]{0:T(256)(128)(2,1)S(1)}, bf16[12]{0:T(256)(128)(2,1)}, u32[]{:S(2)}) copy-start(bf16[12]{0:T(256)(128)(2,1)} %param.27) | copy-start | bytes 76
  52.5 65.6 %copy-start.44 = (bf16[12]{0:T(256)(128)(2,1)S(1)}, bf16[12]{0:T(256)(128)(2,1)}, u32[]{:S(2)}) copy-start(bf16[12]{0:T(256)(128)(2,1)} %param.28) | copy-start | bytes 76
  52.5 65.6 %copy-start.45 = (bf16[12]{0:T(256)(128)(2,1)S(1)}, bf16[12]{0:T(256)(128)(2,1)}, u32[]{:S(2)}) copy-start(bf16[12]{0:T(256)(128)(2,1)} %param.29) | copy-start | bytes 76
  52.6 65.6 %copy-start.46 = (bf16[12]{0:T(256)(128)(2,1)S(1)}, bf16[12]{0:T(256)(128)(2,1)}, u32[]{:S(2)}) copy-start(bf16[12]{0:T(256)(128)(2,1)} %param.33) | copy-start | bytes 76
  52.6 65.6 %copy-start.47 = (bf16[12]{0:T(256)(128)(2,1)S(1)}, bf16[12]{0:T(256)(128)(2,1)}, u32[]{:S(2)}) copy-start(bf16[12]{0:T(256)(128)(2,1)} %param.34) | copy-start | bytes 76
  52.6 65.6 %copy-start.48 = (bf16[12]{0:T(256)(128)(2,1)S(1)}, bf16[12]{0:T(256)(128)(2,1)}, u32[]{:S(2)}) copy-start(bf16[12]{0:T(256)(128)(2,1)} %param.35) | copy-start | bytes 76
  52.6 65.6 %copy-start.49 = (bf16[12]{0:T(256)(128)(2,1)S(1)}, bf16[12]{0:T(256)(128)(2,1)}, u32[]{:S(2)}) copy-start(bf16[12]{0:T(256)(128)(2,1)} %param.39) | copy-start | bytes 76
  52.6 65.6 %copy-start.50 = (bf16[12]{0:T(256)(128)(2,1)S(1)}, bf16[12]{0:T(256)(128)(2,1)}, u32[]{:S(2)}) copy-start(bf16[12]{0:T(256)(128)(2,1)} %param.40) | copy-start | bytes 76
  52.6 65.6 %copy-start.51 = (bf16[12]{0:T(256)(128)(2,1)S(1)}, bf16[12]{0:T(256)(128)(2,1)}, u32[]{:S(2)}) copy-start(bf16[12]{0:T(256)(128)(2,1)} %param.41) | copy-start | bytes 76
  52.7 64.9 %collective-permute-start.15 = (bf16[4,96,1920]{2,1,0:T(8,128)(2,1)S(1)}, bf16[4,96,1920]{2,1,0:T(8,128)(2,1)}, u32[]{:S(2)}, u32[]{:S(2)}) collective-permute-start(bf16[4,96,1920]{2,1,0:T(8,128)(2,1)S(1)} %pad_maximum_fusion.1.refs_8_), channel_id=1, source_target_pairs={{0,64},{1,65},{2,66},{3,67},{4,68},{5,69},{6,70},{7,71},{8,72},{9,... | collective-permute-start | bytes 4423688 | tf_op jit(solution)/shard_map/ppermute | solution.py:496
  55.7 57.8 %collective-permute-start.4 = (bf16[96,1536]{1,0:T(8,128)(2,1)S(1)}, bf16[96,1536]{1,0:T(8,128)(2,1)S(1)}, u32[]{:S(2)}, u32[]{:S(2)}) collective-permute-start(bf16[96,1536]{1,0:T(8,128)(2,1)S(1)} %get-tuple-element.175), channel_id=1, source_target_pairs={{0,64},{1,65},{2,66},{3,67},{4,68},{5,69},{6,70},{7,71},{8,72},{9,... | collective-permute-start | bytes 884744 | tf_op jit(solution)/shard_map/ppermute | solution.py:496
  114.3 21.5 %collective-permute-start.6 = (bf16[2,96,1536]{2,1,0:T(8,128)(2,1)}, bf16[2,96,1536]{2,1,0:T(8,128)(2,1)}, u32[]{:S(2)}, u32[]{:S(2)}) collective-permute-start(bf16[2,96,1536]{2,1,0:T(8,128)(2,1)} %pad_maximum_fusion.2.refs_0_), channel_id=1, source_target_pairs={{0,32},{1,33},{2,34},{3,35},{4,36},{5,37},{6,38},{7,39},{8,40},{9,... | collective-permute-start | bytes 1769480 | tf_op jit(solution)/shard_map/ppermute | solution.py:496
  117.5 388.1 %copy-start.2 = (bf16[1,4,197,768]{3,2,1,0:T(8,128)(2,1)}, bf16[1,4,197,768]{3,2,1,0:T(8,128)(2,1)S(1)}, u32[]{:S(2)}) copy-start(bf16[1,4,197,768]{3,2,1,0:T(8,128)(2,1)S(1)} %copy.84) | copy-start | bytes 3631108
  117.5 46.9 %collective-permute-start.16 = (bf16[4,96,1920]{2,1,0:T(8,128)(2,1)S(1)}, bf16[4,96,1920]{2,1,0:T(8,128)(2,1)}, u32[]{:S(2)}, u32[]{:S(2)}) collective-permute-start(bf16[4,96,1920]{2,1,0:T(8,128)(2,1)S(1)} %pad_maximum_fusion.1.refs_8_), channel_id=1, source_target_pairs={{0,2},{1,3},{2,0},{3,1},{4,6},{5,7},{6,4},{7,5},{8,10},{9,11},{10,... | collective-permute-start | bytes 4423688 | tf_op jit(solution)/shard_map/ppermute | solution.py:496
  117.6 46.8 %collective-permute-start.17 = (bf16[4,96,1920]{2,1,0:T(8,128)(2,1)}, bf16[4,96,1920]{2,1,0:T(8,128)(2,1)}, u32[]{:S(2)}, u32[]{:S(2)}) collective-permute-start(bf16[4,96,1920]{2,1,0:T(8,128)(2,1)} %collective-permute-done.15.refs_9_), channel_id=1, source_target_pairs={{0,2},{1,3},{2,0},{3,1},{4,6},{5,7},{6,4},{7,5},{8,10},{9,11},{10,... | collective-permute-start | bytes 4423688 | tf_op jit(solution)/shard_map/ppermute | solution.py:496
  118.4 39.1 %collective-permute-start.7 = (bf16[2,96,1536]{2,1,0:T(8,128)(2,1)}, bf16[2,96,1536]{2,1,0:T(8,128)(2,1)}, u32[]{:S(2)}, u32[]{:S(2)}) collective-permute-start(bf16[2,96,1536]{2,1,0:T(8,128)(2,1)} %pad_maximum_fusion.2.refs_0_), channel_id=1, source_target_pairs={{0,48},{1,49},{2,50},{3,51},{4,52},{5,53},{6,54},{7,55},{8,56},{9,... | collective-permute-start | bytes 1769480 | tf_op jit(solution)/shard_map/ppermute | solution.py:496
  119.6 38.3 %collective-permute-start.5 = (bf16[2,96,1536]{2,1,0:T(8,128)(2,1)}, bf16[2,96,1536]{2,1,0:T(8,128)(2,1)}, u32[]{:S(2)}, u32[]{:S(2)}) collective-permute-start(bf16[2,96,1536]{2,1,0:T(8,128)(2,1)} %pad_maximum_fusion.2.refs_0_), channel_id=1, source_target_pairs={{0,16},{1,17},{2,18},{3,19},{4,20},{5,21},{6,22},{7,23},{8,24},{9,... | collective-permute-start | bytes 1769480 | tf_op jit(solution)/shard_map/ppermute | solution.py:496
  135.8 22.3 %collective-permute-start.8 = (bf16[2,96,1536]{2,1,0:T(8,128)(2,1)}, bf16[2,96,1536]{2,1,0:T(8,128)(2,1)}, u32[]{:S(2)}, u32[]{:S(2)}) collective-permute-start(bf16[2,96,1536]{2,1,0:T(8,128)(2,1)} %pad_maximum_fusion.2.refs_0_), channel_id=1, source_target_pairs={{0,2},{1,3},{2,0},{3,1},{4,6},{5,7},{6,4},{7,5},{8,10},{9,11},{10,... | collective-permute-start | bytes 1769480 | tf_op jit(solution)/shard_map/ppermute | solution.py:496
  136.7 19.6 %all-to-all-start = ((bf16[64,32,128]{2,1,0:T(8,128)(2,1)}), bf16[64,32,128]{2,1,0:T(8,128)(2,1)}, u32[]{:S(2)}, u32[]{:S(2)}) async-start(bf16[64,32,128]{2,1,0:T(8,128)(2,1)} %broadcast_in_dim.25), calls=%async_computation | async-start | bytes 1048576 | tf_op jit(solution)/shard_map/all_to_all | solution.py:500
  157.6 6.9 collective-permute-start.10
  157.9 6.5 collective-permute-start.11
  158.1 6.3 collective-permute-start.9
  163.9 329.0 %copy-start.6 = (bf16[256,768]{1,0:T(8,128)(2,1)}, bf16[256,768]{1,0:T(8,128)(2,1)S(1)}, u32[]{:S(2)}) copy-start(bf16[256,768]{1,0:T(8,128)(2,1)S(1)} %reshape.309.cls_ref) | copy-start | bytes 1179652
  164.4 341.2 %copy-start.4 = (f32[24,768]{1,0:T(8,128)}, f32[24,768]{1,0:T(8,128)S(1)}, u32[]{:S(2)}) copy-start(f32[24,768]{1,0:T(8,128)S(1)} %pad_convert_fusion.vec_ref) | copy-start | bytes 221188
  626.8 68.4 %collective-permute-start.22 = (bf16[384,3072]{1,0:T(8,128)(2,1)}, bf16[384,3072]{1,0:T(8,128)(2,1)}, u32[]{:S(2)}, u32[]{:S(2)}) collective-permute-start(bf16[384,3072]{1,0:T(8,128)(2,1)} %pad_maximum_fusion), channel_id=1, source_target_pairs={{0,2},{1,3},{2,0},{3,1},{4,6},{5,7},{6,4},{7,5},{8,10},{9,11},{10,... | collective-permute-start | bytes 7077896 | tf_op jit(solution)/shard_map/ppermute | solution.py:496
  628.6 17.7 %all-to-all-start.1 = ((bf16[64,4,768]{2,1,0:T(4,128)(2,1)}), bf16[64,4,768]{2,1,0:T(4,128)(2,1)}, u32[]{:S(2)}, u32[]{:S(2)}) async-start(bf16[64,4,768]{2,1,0:T(4,128)(2,1)} %broadcast_in_dim.53), calls=%async_computation.1 | async-start | bytes 786432 | tf_op jit(solution)/shard_map/all_to_all | solution.py:500
  637.4 71.9 %collective-permute-start.20 = (bf16[384,3072]{1,0:T(8,128)(2,1)}, bf16[384,3072]{1,0:T(8,128)(2,1)}, u32[]{:S(2)}, u32[]{:S(2)}) collective-permute-start(bf16[384,3072]{1,0:T(8,128)(2,1)} %get-tuple-element.77), channel_id=1, source_target_pairs={{0,2},{1,3},{2,0},{3,1},{4,6},{5,7},{6,4},{7,5},{8,10},{9,11},{10,... | collective-permute-start | bytes 7077896 | tf_op jit(solution)/shard_map/ppermute | solution.py:496
  637.4 71.9 %collective-permute-start.21 = (bf16[4,4,2,48,768]{4,3,2,1,0:T(8,128)(2,1)}, bf16[4,4,2,48,768]{4,3,2,1,0:T(8,128)(2,1)}, u32[]{:S(2)}, u32[]{:S(2)}) collective-permute-start(bf16[4,4,2,48,768]{4,3,2,1,0:T(8,128)(2,1)} %get-tuple-element.79), channel_id=1, source_target_pairs={{0,2},{1,3},{2,0},{3,1},{4,6},{5,7},{6,4},{7,5},{8,10},{9,11},{10,... | collective-permute-start | bytes 7077896 | tf_op jit(solution)/shard_map/ppermute | solution.py:496
  687.8 16.9 %all-to-all-start.2 = ((f32[64,1,256]{2,1,0:T(1,128)}), f32[64,1,256]{2,1,0:T(1,128)}, u32[]{:S(2)}, u32[]{:S(2)}) async-start(f32[64,1,256]{2,1,0:T(1,128)} %all_to_all.20), calls=%async_computation.2 | async-start | bytes 131072 | tf_op jit(solution)/shard_map/all_to_all | solution.py:711
  704.7 38.2 %all-to-all-start.4 = ((bf16[16,24,3072]{2,1,0:T(8,128)(2,1)}), bf16[16,24,3072]{2,1,0:T(8,128)(2,1)}, u32[]{:S(2)}, u32[]{:S(2)}) async-start(bf16[16,24,3072]{2,1,0:T(8,128)(2,1)} %bitcast.66), calls=%async_computation.4 | async-start | bytes 4718592 | tf_op jit(solution)/shard_map/all_to_all | solution.py:596
  742.9 74.4 %all-to-all-start.3 = ((bf16[16,24,6144]{2,1,0:T(8,128)(2,1)}), bf16[16,24,6144]{2,1,0:T(8,128)(2,1)}, u32[]{:S(2)}, u32[]{:S(2)}) async-start(bf16[16,24,6144]{2,1,0:T(8,128)(2,1)} %copy-done.1), calls=%async_computation.3 | async-start | bytes 9437184 | tf_op jit(solution)/shard_map/all_to_all | solution.py:596
  750.3 7.5 collective-permute-start.19
  754.8 5.0 collective-permute-start.18
  820.6 9.3 %collective-permute-start.27 = (bf16[48,768]{1,0:T(8,128)(2,1)S(1)}, bf16[48,768]{1,0:T(8,128)(2,1)S(1)}, u32[]{:S(2)}, u32[]{:S(2)}) collective-permute-start(bf16[48,768]{1,0:T(8,128)(2,1)S(1)} %get-tuple-element.195), channel_id=1, source_target_pairs={{0,64},{1,65},{2,66},{3,67},{4,68},{5,69},{6,70},{7,71},{8,72},{9,... | collective-permute-start | bytes 221192 | tf_op jit(solution)/shard_map/ppermute | solution.py:496
  820.7 9.2 %collective-permute-start.28 = (bf16[48,768]{1,0:T(8,128)(2,1)S(1)}, bf16[48,768]{1,0:T(8,128)(2,1)S(1)}, u32[]{:S(2)}, u32[]{:S(2)}) collective-permute-start(bf16[48,768]{1,0:T(8,128)(2,1)S(1)} %get-tuple-element.195), channel_id=1, source_target_pairs={{0,65},{1,64},{2,67},{3,66},{4,69},{5,68},{6,71},{7,70},{8,73},{9,... | collective-permute-start | bytes 221192 | tf_op jit(solution)/shard_map/ppermute | solution.py:496
  824.8 5.1 collective-permute-start.26
  825.0 10.6 %collective-permute-start.24 = (bf16[12,6144]{1,0:T(8,128)(2,1)S(1)}, bf16[12,6144]{1,0:T(8,128)(2,1)S(1)}, u32[]{:S(2)}, u32[]{:S(2)}) collective-permute-start(bf16[12,6144]{1,0:T(8,128)(2,1)S(1)} %get-tuple-element.189), channel_id=1, source_target_pairs={{0,64},{1,65},{2,66},{3,67},{4,68},{5,69},{6,70},{7,71},{8,72},{9,... | collective-permute-start | bytes 442376 | tf_op jit(solution)/shard_map/ppermute | solution.py:496
  826.5 9.1 %collective-permute-start.25 = (bf16[12,6144]{1,0:T(8,128)(2,1)S(1)}, bf16[12,6144]{1,0:T(8,128)(2,1)S(1)}, u32[]{:S(2)}, u32[]{:S(2)}) collective-permute-start(bf16[12,6144]{1,0:T(8,128)(2,1)S(1)} %get-tuple-element.189), channel_id=1, source_target_pairs={{0,65},{1,64},{2,67},{3,66},{4,69},{5,68},{6,71},{7,70},{8,73},{9,... | collective-permute-start | bytes 442376 | tf_op jit(solution)/shard_map/ppermute | solution.py:496
  829.9 5.7 collective-permute-start.23
  (44 other events, 638.9 us)
Sparse Core Ops, SparseCore 0:
  11.8 126.4 all-gather.1
